TPU v7x, 512 devices: a whole 4x8x8 slice. The times are simulated.
512 devices in a mesh: dp: 64 (over z, x, core), mp: 8 (over y).
Axes of the slice: x: 4, y: 8, z: 8, core: 2. Of those that a mesh axis runs over, the one named last changes fastest.
Arguments:
- grads: bfloat16 [64, 32, 512, 512], P('dp', None, 'mp'), may hold values from -0.5 to 0.5
- slot_blocks: int32 [64, 1], replicated, may hold values from 0 to 31, as said below
- counts: int32 [64], P('dp'), may hold values from 0 to 1, as said below
- left_stat: bfloat16 [64, 1, 512, 512], P('dp', None, 'mp'), may hold values from -6 to 6
- right_stat: bfloat16 [64, 1, 512, 512], P('dp', None, 'mp'), may hold values from -6 to 6
- left_root: bfloat16 [64, 1, 512, 512], P('dp', None, 'mp')
- right_root: bfloat16 [64, 1, 512, 512], P('dp', None, None, 'mp')
Outputs:
- left_new: bfloat16 [64, 1, 512, 512], P('dp', None, 'mp')
- right_new: bfloat16 [64, 1, 512, 512], P('dp', None, 'mp')
- update: bfloat16 [64, 1, 512, 512], P('dp', None, 'mp')
Inputs may be any that keep to these rules, and one draw needn't show every extreme that they name: `slot_blocks`: every block 0 to 31 stands in exactly one live slot (s < counts[o]); ids in slots that are not live are arbitrary. `counts`: some owner has all 1 slots live.
All inputs are finite; a program needn't handle non-finite values.
Results may differ from a plain program's by a relative error of at most 0.0058.
Values may be sent and summed in bfloat16 or wider, within the bound.
No kernel may reach another device: no remote copies, remote signals or barrier semaphores. Data moves between devices by JAX's collectives and lax.ppermute only.
A program may use at most 64 MiB of HBM per device.

v0:
```python
import jax
import jax.numpy as jnp
from jax import lax
from jax.sharding import PartitionSpec as P

BETA = 0.9
RATE = 0.5
EPS = 1e-06


def slot_update(grad_rows, lstat, rstat, lroot, rroot):
    rows, width = grad_rows.shape
    g_rows = grad_rows.astype(jnp.bfloat16)
    offset = lax.axis_index("mp") * rows
    piece = lax.all_gather(g_rows, "mp", axis=0, tiled=True)
    left_part = jnp.dot(g_rows, piece.T, preferred_element_type=jnp.float32)
    own_cols = lax.dynamic_slice_in_dim(piece, offset, rows, 1)
    right_part = lax.dot_general(
        own_cols, piece, (((0,), (0,)), ((), ())), preferred_element_type=jnp.float32
    )
    middle = jnp.dot(piece, rroot, preferred_element_type=jnp.float32)
    piece_float = piece.astype(jnp.float32)
    squares = jnp.sum(piece_float * piece_float)
    gram_left, gram_right, middle, squares = (left_part, right_part, middle, squares)
    middle_low = middle.astype(jnp.bfloat16)
    pre = jnp.dot(
        lroot,
        lax.all_gather(middle_low, "mp", axis=1, tiled=True),
        preferred_element_type=jnp.float32,
    )
    pre_squares = lax.psum(jnp.sum(pre * pre), "mp")
    cells = float(width * width)
    scale = jnp.sqrt(squares / cells) / jnp.sqrt(pre_squares / cells + EPS)
    new_left = (BETA * lstat.astype(jnp.float32) + (1.0 - BETA) * gram_left).astype(jnp.bfloat16)
    new_right = (BETA * rstat.astype(jnp.float32) + (1.0 - BETA) * gram_right).astype(jnp.bfloat16)
    new_update = (-RATE * scale * pre).astype(jnp.bfloat16)
    return (new_left, new_right, new_update)


def on_device(grads, slot_blocks, counts, left_stat, right_stat, left_root, right_root):
    terms = grads[0].astype(jnp.float32)
    owner = lax.axis_index("dp")
    mine_ids = lax.dynamic_index_in_dim(slot_blocks, owner, 0, keepdims=False)
    summed = lax.psum(terms, "dp")
    mine = jnp.take(summed, mine_ids, axis=0)
    live_count = counts[0]
    lstats = left_stat[0]
    rstats = right_stat[0]
    lroots = left_root[0]
    rroots = right_root[0]
    blank = jnp.zeros(lstats.shape, jnp.bfloat16)
    new_left, new_right, new_update = slot_update(
        mine[0], lstats[0], rstats[0], lroots[0], rroots[0]
    )
    alive = 0 < live_count
    left_list = [jnp.where(alive, new_left, lstats[0])]
    right_list = [jnp.where(alive, new_right, rstats[0])]
    update_list = [jnp.where(alive, new_update, blank[0])]
    out_left = jnp.stack(left_list)
    out_right = jnp.stack(right_list)
    out_update = jnp.stack(update_list)
    return (out_left[None], out_right[None], out_update[None])


def solution(mesh):
    return jax.shard_map(
        on_device,
        mesh=mesh,
        in_specs=(
            P("dp", None, "mp", None),
            P(),
            P("dp"),
            P("dp", None, "mp", None),
            P("dp", None, "mp", None),
            P("dp", None, "mp", None),
            P("dp", None, None, "mp"),
        ),
        out_specs=(P("dp", None, "mp", None), P("dp", None, "mp", None), P("dp", None, "mp", None)),
        check_vma=False,
    )
```

profile of v0, /device:TPU:8, one launch (start us, length us, event | category | flops | bytes accessed | tf_op | source)
XLA Modules:
  0.0 383.0 jit_solution(12029413759382485439)
XLA Ops:
  0.6 0.0 copy-start
  0.6 4.1 %bitcast_convert_fusion = f32[32,64,512]{2,1,0:T(8,128)} fusion(bf16[1,32,64,512]{3,2,1,0:T(8,128)(2,1)} %param.7), kind=kLoop, calls=%fused_computation | loop fusion | flops 1048576 | bytes 6291456 | tf_op jit(solution)/shard_map/convert_element_type | solution.py:41
  4.8 0.0 copy-start.4
  4.8 0.0 copy-start.1
  4.8 0.0 copy-start.2
  4.8 301.3 %all-reduce.1 = bf16[32,64,512]{2,1,0:T(8,128)(2,1)S(1)} all-reduce(f32[32,64,512]{2,1,0:T(8,128)} %bitcast_convert_fusion), channel_id=1, replica_groups=mesh['dp'=64,'mp'=8] {'dp'}, use_global_device_ids=true, to_apply=%region_0.1 | all-reduce | flops 1048576 | bytes 6291456 | tf_op jit(solution)/shard_map/psum | solution.py:44
  306.1 0.0 copy-start.3
  306.1 0.0 copy-done.4
  306.1 0.6 constant_dynamic-slice_fusion
  308.6 26.0 %all-gather = bf16[1,512,512]{2,1,0:T(8,128)(2,1)S(1)} all-gather(bf16[1,64,512]{2,1,0:T(8,128)(2,1)S(1)} %fusion.13), channel_id=2, replica_groups=mesh['dp'=64,'mp'=8] {'mp'}, dimensions={1}, use_global_device_ids=true | all-gather | bytes 589824 | tf_op jit(solution)/shard_map/all_gather | solution.py:15
  335.2 0.0 copy-done.1
  335.3 0.9 fusion.7
  336.2 0.0 copy-done.2
  336.2 0.9 fusion.5
  337.1 0.0 copy-done.3
  337.1 0.3 convolution_convert_fusion
  337.4 25.2 %all_gather.7 = bf16[512,512]{0,1:T(8,128)(2,1)S(1)} all-gather(bf16[512,64]{0,1:T(8,128)(2,1)S(1)} %convolution_convert_fusion), channel_id=1, replica_groups=mesh['dp'=64,'mp'=8] {'mp'}, dimensions={1}, use_global_device_ids=true | all-gather | bytes 589824 | tf_op jit(solution)/shard_map/all_gather | solution.py:28
  362.6 0.0 copy-done
  362.6 0.9 multiply_reduce_fusion.1
  363.6 0.9 multiply_reduce_fusion
  365.0 16.6 %psum.15 = f32[]{:T(128)} all-reduce(f32[]{:T(128)} %get-tuple-element.14), channel_id=1, replica_groups=mesh['dp'=64,'mp'=8] {'mp'}, use_global_device_ids=true, to_apply=%region_3.4 | all-reduce | flops 1 | bytes 8 | tf_op jit(solution)/shard_map/psum | solution.py:31
  382.3 0.6 fusion.15
  (1 shorter events, 0.0 us)
Async XLA Ops:
  0.6 362.0 %copy-start = (bf16[1,1,64,512]{3,2,1,0:T(8,128)(2,1)S(1)}, bf16[1,1,64,512]{3,2,1,0:T(8,128)(2,1)}, u32[]{:S(2)}) copy-start(bf16[1,1,64,512]{3,2,1,0:T(8,128)(2,1)} %param.12) | copy-start | bytes 196612
  4.8 301.3 %copy-start.4 = (s32[64,1]{0,1:T(1,128)S(1)}, s32[64,1]{0,1:T(1,128)}, u32[]{:S(2)}) copy-start(s32[64,1]{0,1:T(1,128)} %param.8) | copy-start | bytes 772
  4.8 330.5 %copy-start.1 = (bf16[1,1,64,512]{3,2,1,0:T(8,128)(2,1)S(1)}, bf16[1,1,64,512]{3,2,1,0:T(8,128)(2,1)}, u32[]{:S(2)}) copy-start(bf16[1,1,64,512]{3,2,1,0:T(8,128)(2,1)} %param.10) | copy-start | bytes 196612
  4.8 331.4 %copy-start.2 = (bf16[1,1,64,512]{3,2,1,0:T(8,128)(2,1)S(1)}, bf16[1,1,64,512]{3,2,1,0:T(8,128)(2,1)}, u32[]{:S(2)}) copy-start(bf16[1,1,64,512]{3,2,1,0:T(8,128)(2,1)} %param.11) | copy-start | bytes 196612
  306.1 31.1 %copy-start.3 = (bf16[1,1,512,64]{2,3,1,0:T(8,128)(2,1)S(1)}, bf16[1,1,512,64]{2,3,1,0:T(8,128)(2,1)}, u32[]{:S(2)}) copy-start(bf16[1,1,512,64]{2,3,1,0:T(8,128)(2,1)} %param.13) | copy-start | bytes 196612
where the time goes:
time: 383 us
  blocking collectives  369 us (96%)
  other arithmetic  5.64 us (1%)
  between operations  4.6 us (1%)
    psum x1, blocking collectives, on_device(): summed = lax.psum(terms, 'dp')  301 us
    all_gather x1, blocking collectives, slot_update(): piece = lax.all_gather(g_rows, 'mp', axis=0, tiled=True)  26 us
    all_gather x1, blocking collectives, slot_update(): lax.all_gather(middle_low, 'mp', axis=1, tiled=True)  25.2 us
    psum x1, blocking collectives, slot_update(): pre_squares = lax.psum(jnp.sum(pre * pre), 'mp')  16.6 us

commit v1 on v0

v1 whole, which is shorter than its diff:
```python
import functools

import jax
import jax.numpy as jnp
from jax import lax
from jax.experimental import pallas as pl
from jax.experimental.pallas import tpu as pltpu
from jax.sharding import Mesh
from jax.sharding import PartitionSpec as P

BETA = 0.9
RATE = 0.5
EPS = 1e-06
NZ, NX, NC = 8, 4, 2
F32 = jnp.float32
BF16 = jnp.bfloat16
DP = ("z", "x", "c")


def route_kernel(ids_ref, terms_ref, out_ref, held_ref):
    nblk = held_ref.shape[0]
    total = terms_ref[0].astype(F32)
    for i in range(1, NX):
        total += terms_ref[i].astype(F32)
    held_ref[...] = total.astype(BF16)

    def body(i, carry):
        for k in range(8):
            o = i * 8 + k
            b = jnp.clip(ids_ref[o], 0, nblk - 1)
            out_ref[o] = held_ref[b]
        return carry

    lax.fori_loop(0, out_ref.shape[0] // 8, body, 0)


def collect_kernel(terms_ref, out_ref):
    n_out, rows = out_ref.shape[0], terms_ref.shape[1]
    for x in range(NX):
        for c in range(NC):
            total = terms_ref[x * NC + c].astype(F32)
            for z in range(1, NZ):
                total += terms_ref[(z * NX + x) * NC + c].astype(F32)
            low = total.astype(BF16)
            for k in range(n_out):
                out_ref[k, pl.ds(c * rows, rows), pl.ds(x * 128, 128)] = low


def finish_kernel(live_ref, g_ref, lstat_ref, rstat_ref, roots_ref, left_ref, right_ref, update_ref, gram_ref, pre_ref):
    n_mp, _, rows, width = roots_ref.shape
    m = live_ref[1]
    alive = live_ref[0] > 0
    mine = pl.ds(pl.multiple_of(m * rows, rows), rows)
    g = g_ref[...]
    cells = float(width * width)
    nt = (((1,), (1,)), ((), ()))
    tn = (((0,), (0,)), ((), ()))
    gram_left = lax.dot_general(g_ref[mine, :], g, nt, preferred_element_type=F32)
    lstat, rstat = lstat_ref[...], rstat_ref[...]
    new_left = (BETA * lstat.astype(F32) + (1.0 - BETA) * gram_left).astype(BF16)
    left_ref[...] = jnp.where(alive, new_left, lstat)
    gram_ref[...] = lax.dot_general(g, g, tn, preferred_element_type=F32)
    new_right = (BETA * rstat.astype(F32) + (1.0 - BETA) * gram_ref[mine, :]).astype(BF16)
    right_ref[...] = jnp.where(alive, new_right, rstat)
    lroot = roots_ref[:, 0].reshape(width, width)
    rroot_t = roots_ref[:, 1].reshape(width, width)
    middle = lax.dot_general(g, rroot_t, nt, preferred_element_type=F32).astype(BF16)
    pre = jnp.dot(lroot, middle, preferred_element_type=F32)
    pre_ref[...] = pre
    g_float = g.astype(F32)
    squares = jnp.sum(g_float * g_float)
    pre_squares = jnp.sum(pre * pre)
    top = jnp.full((1, 1), squares, F32) / cells
    bottom = jnp.full((1, 1), pre_squares, F32) / cells + EPS
    scale = jnp.sqrt(top) / jnp.sqrt(bottom)
    new_update = (-RATE * scale * pre_ref[mine, :]).astype(BF16)
    update_ref[...] = jnp.where(alive, new_update, jnp.zeros_like(new_update))


def on_device(grads, slot_blocks, counts, left_stat, right_stat, left_root, right_root):
    terms = grads[0]
    nblk, rows, width = terms.shape
    half, quarter = rows // NC, width // NX
    vmem = pl.BlockSpec(memory_space=pltpu.VMEM)
    smem = pl.BlockSpec(memory_space=pltpu.SMEM)
    limit = pltpu.CompilerParams(vmem_limit_bytes=48 * 1024 * 1024)
    n_mp = width // rows

    roots = jnp.stack([left_root[0, 0], right_root[0, 0].T])
    roots_all = lax.all_gather(roots, "mp", axis=0)

    core = lax.axis_index("c")
    halves = terms.reshape(nblk, NC, half, width)
    away = lax.dynamic_index_in_dim(halves, 1 - core, 1, keepdims=False)
    here = lax.dynamic_index_in_dim(halves, core, 1, keepdims=False)
    come = lax.ppermute(away, "c", [(0, 1), (1, 0)])
    pair = (here.astype(F32) + come.astype(F32)).astype(BF16)
    pair = pair.reshape(nblk, half, NX, quarter).transpose(2, 0, 1, 3)
    along_x = lax.all_to_all(pair, "x", 0, 0, tiled=True)

    owners = slot_blocks.shape[0]
    routed = pl.pallas_call(
        route_kernel,
        out_shape=jax.ShapeDtypeStruct((owners, half, quarter), BF16),
        in_specs=[smem, vmem],
        out_specs=vmem,
        scratch_shapes=[pltpu.VMEM((nblk, half, quarter), BF16)],
        compiler_params=limit,
    )(slot_blocks[:, 0], along_x)
    owned = lax.all_to_all(routed, DP, 0, 0, tiled=True)
    copies = pl.pallas_call(
        collect_kernel,
        out_shape=jax.ShapeDtypeStruct((n_mp, rows, width), BF16),
        in_specs=[vmem],
        out_specs=vmem,
        compiler_params=limit,
    )(owned)
    g = lax.all_to_all(copies, "mp", 0, 0, tiled=True).reshape(width, width)

    live = jnp.stack([counts[0], lax.axis_index("mp").astype(jnp.int32)])
    shape = jax.ShapeDtypeStruct((rows, width), BF16)
    outs = pl.pallas_call(
        finish_kernel,
        out_shape=(shape, shape, shape),
        in_specs=[smem, vmem, vmem, vmem, vmem],
        out_specs=(vmem, vmem, vmem),
        scratch_shapes=[pltpu.VMEM((width, width), F32), pltpu.VMEM((width, width), F32)],
        compiler_params=limit,
    )(live, g, left_stat[0, 0], right_stat[0, 0], roots_all)
    return tuple(o[None, None] for o in outs)


def solution(mesh):
    fine = Mesh(mesh.devices.reshape(NZ, NX, NC, mesh.devices.shape[1]), ("z", "x", "c", "mp"))
    rows = P(DP, None, "mp", None)
    return jax.shard_map(
        on_device,
        mesh=fine,
        in_specs=(rows, P(), P(DP), rows, rows, rows, P(DP, None, None, "mp")),
        out_specs=(rows, rows, rows),
        check_vma=False,
    )
```

time: 383 us -> 110 us (0.29)
  the two profiles are of different devices: /device:TPU:8 before, /device:TPU:2 now
where the time goes in v1:
time: 110 us; the launch traced here: 109 us
  waiting for transfers between devices  43.3 us (39%)
  blocking collectives  22.7 us (21%)
  starting transfers between devices  18.1 us (16%)
  between operations  14.8 us (13%)
  Pallas kernels  5.29 us (5%)
  local copies, waits for them, and re-layouts  2.71 us (2%)
  other arithmetic  2.23 us (2%)
    all_gather x1, waiting for transfers between devices, on_device(): roots_all = lax.all_gather(roots, 'mp', axis=0)  23.7 us
    all_to_all x1, blocking collectives, on_device(): along_x = lax.all_to_all(pair, 'x', 0, 0, tiled=True)  22.7 us
    all_to_all x1, waiting for transfers between devices, on_device(): owned = lax.all_to_all(routed, DP, 0, 0, tiled=True)  16.8 us
    all_to_all x1, starting transfers between devices, on_device(): owned = lax.all_to_all(routed, DP, 0, 0, tiled=True)  9.08 us
    all_to_all x1, starting transfers between devices, on_device(): g = lax.all_to_all(copies, 'mp', 0, 0, tiled=True).reshape(width, width)  7.1 us
    ppermute x1, waiting for transfers between devices, on_device(): come = lax.ppermute(away, 'c', [(0, 1), (1, 0)])  2.75 us
    pallas_call x1, Pallas kernels, on_device(): pl.pallas_call(finish_kernel, out_shape=(shape, shape, shape), in_specs=[...  2.67 us
  transfers between devices with their start and end apart: 4, of which 3 were waited for; matrix products, arithmetic and copies ran while one was open for 1% of the time, Pallas kernels for 1%

profile of v1, /device:TPU:2, one launch (start us, length us, event | category | flops | bytes accessed | tf_op | source)
XLA Modules:
  0.0 109.1 jit_solution(6713035392172834072)
XLA Ops:
  7.2 0.0 copy-start.4
  7.2 1.5 %dynamic-slice_bitcast_fusion = bf16[32,32,512]{2,1,0:T(8,128)(2,1)S(1)} fusion(bf16[32,2,32,512]{3,2,1,0:T(8,128)(2,1)} %bitcast.36, s32[]{:T(128)S(6)} %select_n.8), kind=kLoop, calls=%fused_computation.4 | loop fusion | bytes 2097156 | tf_op jit(solution)/shard_map/jit(dynamic_index_in_dim)/squeeze | solution.py:94
  8.6 1.9 %collective-permute-start = (bf16[32,32,512]{2,1,0:T(8,128)(2,1)S(1)}, bf16[32,32,512]{2,1,0:T(8,128)(2,1)}, u32[]{:S(2)}, u32[]{:S(2)}) collective-permute-start(bf16[32,32,512]{2,1,0:T(8,128)(2,1)S(1)} %dynamic-slice_bitcast_fusion), channel_id=1, source_target_pairs={{0,8},{8,0},{1,9},{9,1},{2,10},{10,2},{3,11},{11,3},{4,12},{12,4},... | collective-permute-start | bytes 3145736 | tf_op jit(solution)/shard_map/ppermute | solution.py:96
  10.6 0.0 copy-start.3
  10.6 2.7 %collective-permute-done = bf16[32,32,512]{2,1,0:T(8,128)(2,1)} collective-permute-done((bf16[32,32,512]{2,1,0:T(8,128)(2,1)S(1)}, bf16[32,32,512]{2,1,0:T(8,128)(2,1)}, u32[]{:S(2)}, u32[]{:S(2)}) %collective-permute-start) | collective-permute-done | bytes 1048608 | tf_op jit(solution)/shard_map/ppermute | solution.py:96
  13.3 0.0 copy-done.4
  13.3 1.5 %bitcast_bitcast_fusion = bf16[4,32,32,128]{3,2,1,0:T(8,128)(2,1)S(1)} fusion(bf16[32,32,512]{2,1,0:T(8,128)(2,1)} %collective-permute-done, bf16[32,2,32,512]{3,2,1,0:T(8,128)(2,1)S(1)} %bitcast.37, s32[]{:T(128)S(6)} %select_n.7), kind=kLoop, calls=%fused_computation.3 | loop fusion | flops 2097152 | bytes 3145732 | tf_op jit(solution)/shard_map/transpose | solution.py:98
  14.8 0.0 copy-start.5
  14.8 0.0 copy-start.6
  14.9 22.7 %all_to_all.15.terms_ref = bf16[4,32,32,128]{3,2,1,0:T(8,128)(2,1)S(1)} all-to-all(bf16[4,32,32,128]{3,2,1,0:T(8,128)(2,1)S(1)} %bitcast_bitcast_fusion), channel_id=1, replica_groups=mesh['z'=8,'x'=4,'c'=2,'mp'=8] {'x'}, dimensions={0} | all-to-all | bytes 2097152 | tf_op jit(solution)/shard_map/all_to_all | solution.py:99
  37.5 0.0 copy-done.3
  37.5 1.7 %shard_map.94 = bf16[64,32,128]{2,1,0:T(8,128)(2,1)} custom-call(s32[64]{0:T(128)S(1)} %bitcast.35, bf16[4,32,32,128]{3,2,1,0:T(8,128)(2,1)S(1)} %all_to_all.15.terms_ref), custom_call_target="tpu_custom_call" | custom-call | tf_op jit(solution)/shard_map/pallas_call | solution.py:102
  39.2 0.0 copy-start.1
  39.2 0.0 copy-start.2
  39.2 9.1 %all-to-all-start.1 = ((bf16[64,32,128]{2,1,0:T(8,128)(2,1)}), bf16[64,32,128]{2,1,0:T(8,128)(2,1)S(1)}, u32[]{:S(2)}, u32[]{:S(2)}) async-start(bf16[64,32,128]{2,1,0:T(8,128)(2,1)} %shard_map.94), calls=%async_computation.1 | async-start | bytes 1048576 | tf_op jit(solution)/shard_map/all_to_all | solution.py:110
  48.3 0.0 all-gather.3.cloned.1.call-start
  48.4 0.0 copy-done.5
  48.4 0.0 copy-done.6
  48.4 0.7 pad_maximum_fusion
  49.0 0.0 all-gather.3.cloned.1.call-update
  49.1 16.8 %all-to-all-done.1.terms_ref = bf16[64,32,128]{2,1,0:T(8,128)(2,1)S(1)} async-done(((bf16[64,32,128]{2,1,0:T(8,128)(2,1)}), bf16[64,32,128]{2,1,0:T(8,128)(2,1)S(1)}, u32[]{:S(2)}, u32[]{:S(2)}) %all-to-all-start.1) | async-done | bytes 524320 | tf_op jit(solution)/shard_map/all_to_all | solution.py:110
  65.9 0.9 shard_map.95
  66.8 7.1 %all-to-all-start.2 = ((bf16[8,64,512]{2,1,0:T(8,128)(2,1)}), bf16[8,64,512]{2,1,0:T(8,128)(2,1)S(1)}, u32[]{:S(2)}, u32[]{:S(2)}) async-start(bf16[8,64,512]{2,1,0:T(8,128)(2,1)} %shard_map.95), calls=%async_computation.2 | async-start | bytes 1048576 | tf_op jit(solution)/shard_map/all_to_all | solution.py:118
  74.6 0.1 pad_add_fusion.live_ref
  74.6 23.7 %all-gather.3.cloned.1.call-done = bf16[16,64,512]{2,1,0:T(8,128)(2,1)} async-done(((bf16[2,64,512]{2,1,0:T(8,128)(2,1)}), bf16[16,64,512]{2,1,0:T(8,128)(2,1)}) %all-gather.3.cloned.1.call-update) | async-done | bytes 1048592 | tf_op jit(solution)/shard_map/all_gather | solution.py:90
  98.3 0.0 all-to-all-done.2
  98.3 0.0 copy-done.1
  98.3 0.0 copy-done.2
  98.4 0.0 copy-start
  98.4 1.2 %copy-done = bf16[16,64,512]{2,1,0:T(8,128)(2,1)S(1)} copy-done((bf16[16,64,512]{2,1,0:T(8,128)(2,1)S(1)}, bf16[16,64,512]{2,1,0:T(8,128)(2,1)}, u32[]{:S(2)}) %copy-start) | copy-done | bytes 1048600
  99.6 2.7 %shard_map.96 = (bf16[64,512]{1,0:T(8,128)(2,1)}, bf16[64,512]{1,0:T(8,128)(2,1)}, bf16[64,512]{1,0:T(8,128)(2,1)}) custom-call(s32[2]{0:T(128)S(1)} %pad_add_fusion.live_ref, bf16[512,512]{1,0:T(8,128)(2,1)S(1)} %bitcast.31, bf16[64,512]{1,0:T(8,128)(2,1)S(1)} %bitcast.33, bf16[64,512]{1,0:T(8,128)(2,1)S(1)} %bitcast.34, bf16[8,2,64,512]{3,2,1,0:T(8,128)(2,1)S(1)} %bitcast.32), custom_call_target="tpu_custom_call" | custom-call | tf_op jit(solution)/shard_map/pallas_call | solution.py:122
Async XLA Ops:
  7.2 6.2 %copy-start.4 = (bf16[1,32,64,512]{3,2,1,0:T(8,128)(2,1)S(1)}, bf16[1,32,64,512]{3,2,1,0:T(8,128)(2,1)}, u32[]{:S(2)}) copy-start(bf16[1,32,64,512]{3,2,1,0:T(8,128)(2,1)} %param.7) | copy-start | bytes 6291460
  8.6 4.7 %collective-permute-start = (bf16[32,32,512]{2,1,0:T(8,128)(2,1)S(1)}, bf16[32,32,512]{2,1,0:T(8,128)(2,1)}, u32[]{:S(2)}, u32[]{:S(2)}) collective-permute-start(bf16[32,32,512]{2,1,0:T(8,128)(2,1)S(1)} %dynamic-slice_bitcast_fusion), channel_id=1, source_target_pairs={{0,8},{8,0},{1,9},{9,1},{2,10},{10,2},{3,11},{11,3},{4,12},{12,4},... | collective-permute-start | bytes 3145736 | tf_op jit(solution)/shard_map/ppermute | solution.py:96
  10.6 27.0 %copy-start.3 = (s32[64,1]{0,1:T(1,128)S(1)}, s32[64,1]{0,1:T(1,128)}, u32[]{:S(2)}) copy-start(s32[64,1]{0,1:T(1,128)} %param.8) | copy-start | bytes 772
  14.8 33.5 %copy-start.5 = (bf16[1,1,512,64]{2,3,1,0:T(8,128)(2,1)S(1)}, bf16[1,1,512,64]{2,3,1,0:T(8,128)(2,1)}, u32[]{:S(2)}) copy-start(bf16[1,1,512,64]{2,3,1,0:T(8,128)(2,1)} %param.13) | copy-start | bytes 196612
  14.8 33.5 %copy-start.6 = (bf16[1,1,64,512]{3,2,1,0:T(8,128)(2,1)S(1)}, bf16[1,1,64,512]{3,2,1,0:T(8,128)(2,1)}, u32[]{:S(2)}) copy-start(bf16[1,1,64,512]{3,2,1,0:T(8,128)(2,1)} %param.12) | copy-start | bytes 196612
  39.2 59.1 %copy-start.1 = (bf16[1,1,64,512]{3,2,1,0:T(8,128)(2,1)S(1)}, bf16[1,1,64,512]{3,2,1,0:T(8,128)(2,1)}, u32[]{:S(2)}) copy-start(bf16[1,1,64,512]{3,2,1,0:T(8,128)(2,1)} %param.10) | copy-start | bytes 196612
  39.2 59.1 %copy-start.2 = (bf16[1,1,64,512]{3,2,1,0:T(8,128)(2,1)S(1)}, bf16[1,1,64,512]{3,2,1,0:T(8,128)(2,1)}, u32[]{:S(2)}) copy-start(bf16[1,1,64,512]{3,2,1,0:T(8,128)(2,1)} %param.11) | copy-start | bytes 196612
  39.2 26.7 %all-to-all-start.1 = ((bf16[64,32,128]{2,1,0:T(8,128)(2,1)}), bf16[64,32,128]{2,1,0:T(8,128)(2,1)S(1)}, u32[]{:S(2)}, u32[]{:S(2)}) async-start(bf16[64,32,128]{2,1,0:T(8,128)(2,1)} %shard_map.94), calls=%async_computation.1 | async-start | bytes 1048576 | tf_op jit(solution)/shard_map/all_to_all | solution.py:110
  48.3 50.0 %all-gather.3.cloned.1.call-start = ((), (), s32[]{:S(2)}) async-start(), calls=%async_computation.3 | async-start | bytes 1179648 | tf_op jit(solution)/shard_map/all_gather | solution.py:90
  66.8 31.5 %all-to-all-start.2 = ((bf16[8,64,512]{2,1,0:T(8,128)(2,1)}), bf16[8,64,512]{2,1,0:T(8,128)(2,1)S(1)}, u32[]{:S(2)}, u32[]{:S(2)}) async-start(bf16[8,64,512]{2,1,0:T(8,128)(2,1)} %shard_map.95), calls=%async_computation.2 | async-start | bytes 1048576 | tf_op jit(solution)/shard_map/all_to_all | solution.py:118
  98.4 1.2 %copy-start = (bf16[16,64,512]{2,1,0:T(8,128)(2,1)S(1)}, bf16[16,64,512]{2,1,0:T(8,128)(2,1)}, u32[]{:S(2)}) copy-start(bf16[16,64,512]{2,1,0:T(8,128)(2,1)} %all-gather.3.cloned.1.call-done) | copy-start | bytes 3145732
Sparse Core Ops, SparseCore 0:
  51.2 47.0 all-gather.2

commit v2 on v1

v2 whole, which is shorter than its diff:
```python
import jax
import jax.numpy as jnp
from jax import lax
from jax.experimental import pallas as pl
from jax.experimental.pallas import tpu as pltpu
from jax.sharding import Mesh
from jax.sharding import PartitionSpec as P

BETA = 0.9
RATE = 0.5
EPS = 1e-06
NZ, NX, NC = 8, 4, 2
F32 = jnp.float32
BF16 = jnp.bfloat16
BATCH = 8
DP = ("z", "x", "c")
BACK = (0, 1, 7, 2, 6, 3, 5, 4)


def pair_kernel(core_ref, terms_ref, come_ref, out_ref):
    total = (terms_ref[:, 0].astype(F32) + come_ref[...].astype(F32)).astype(BF16)
    for x in range(NX):
        out_ref[x] = total[:, :, x * 128 : (x + 1) * 128]


def route_kernel(ids_ref, terms_ref, out_ref, held_ref):
    nblk = held_ref.shape[0]
    total = terms_ref[0].astype(F32)
    for x in range(1, NX):
        total += terms_ref[x].astype(F32)
    held_ref[...] = total.astype(BF16)

    def body(i, carry):
        for k in range(8):
            o = i * 8 + k
            b = jnp.clip(ids_ref[o], 0, nblk - 1)
            out_ref[o] = held_ref[b]
        return carry

    lax.fori_loop(0, out_ref.shape[0] // 8, body, 0)


def collect_kernel(terms_ref, out_ref):
    n_out, rows = out_ref.shape[0], terms_ref.shape[1]
    for x in range(NX):
        for c in range(NC):
            total = terms_ref[x * NC + c].astype(F32)
            for z in range(1, NZ):
                total += terms_ref[(z * NX + x) * NC + c].astype(F32)
            low = total.astype(BF16)
            for k in range(n_out):
                out_ref[k, pl.ds(c * rows, rows), pl.ds(x * 128, 128)] = low


def finish_kernel(live_ref, parts_ref, lstat_ref, rstat_ref, *refs):
    n_mp, rows, width = parts_ref.shape
    root_refs, refs = refs[:n_mp], refs[n_mp:]
    left_ref, right_ref, update_ref, g_ref, gram_ref, lroot_ref, rroot_ref = refs
    m = live_ref[1]
    alive = live_ref[0] > 0
    mine = pl.ds(pl.multiple_of(m * rows, rows), rows)
    for k in range(n_mp):
        g_ref[pl.ds(k * rows, rows), :] = parts_ref[k]
    g = g_ref[...]
    cells = float(width * width)
    nt = (((1,), (1,)), ((), ()))
    tn = (((0,), (0,)), ((), ()))
    gram_left = lax.dot_general(g_ref[mine, :], g, nt, preferred_element_type=F32)
    lstat, rstat = lstat_ref[...], rstat_ref[...]
    new_left = (BETA * lstat.astype(F32) + (1.0 - BETA) * gram_left).astype(BF16)
    left_ref[...] = jnp.where(alive, new_left, lstat)
    gram_ref[...] = lax.dot_general(g, g, tn, preferred_element_type=F32)
    new_right = (BETA * rstat.astype(F32) + (1.0 - BETA) * gram_ref[mine, :]).astype(BF16)
    right_ref[...] = jnp.where(alive, new_right, rstat)
    for i, (ref, back) in enumerate(zip(root_refs, BACK)):
        lroot_ref[pl.ds(i * rows, rows), :] = ref[0]
        place = lax.rem(m + n_mp - back, n_mp) * rows
        rroot_ref[pl.ds(pl.multiple_of(place, rows), rows), :] = ref[1]
    middle = lax.dot_general(g, rroot_ref[...], nt, preferred_element_type=F32).astype(BF16)
    pre = jnp.dot(lroot_ref[...], middle, preferred_element_type=F32)
    g_float = g.astype(F32)
    squares = jnp.sum(g_float * g_float)
    pre_squares = jnp.sum(pre * pre)
    top = jnp.full((1, 1), squares, F32) / cells
    bottom = jnp.full((1, 1), pre_squares, F32) / cells + EPS
    scale = jnp.sqrt(top) / jnp.sqrt(bottom)
    new_update = (-RATE * scale * pre[:rows]).astype(BF16)
    update_ref[...] = jnp.where(alive, new_update, jnp.zeros_like(new_update))


VMEM = pl.BlockSpec(memory_space=pltpu.VMEM)
SMEM = pl.BlockSpec(memory_space=pltpu.SMEM)
LIMIT = pltpu.CompilerParams(vmem_limit_bytes=16 * 1024 * 1024)


def kernel_call(kernel, out_shape, scratch, scalars, *arrays):
    return pl.pallas_call(
        kernel,
        out_shape=out_shape,
        in_specs=[SMEM] * len(scalars) + [VMEM] * len(arrays),
        out_specs=jax.tree.map(lambda _: VMEM, out_shape),
        scratch_shapes=scratch,
        compiler_params=LIMIT,
    )(*scalars, *arrays)


def bf16(*shape):
    return jax.ShapeDtypeStruct(shape, BF16)


def on_device(grads, slot_blocks, counts, left_stat, right_stat, left_root, right_root):
    terms = grads[0]
    nblk, rows, width = terms.shape
    n_mp = width // rows
    core = lax.axis_index("c")

    half, quarter = rows // NC, width // NX
    halves = terms.reshape(nblk, NC, half, width)
    away = lax.dynamic_index_in_dim(halves, 1 - core, 1, keepdims=False)
    come = lax.ppermute(away, "c", [(0, 1), (1, 0)])

    def shift(a, k):
        return lax.ppermute(a, "mp", [(i, (i + k) % n_mp) for i in range(n_mp)])

    own = jnp.stack([left_root[0, 0], right_root[0, 0].T])
    pairs = pl.pallas_call(
        pair_kernel,
        grid_spec=pltpu.PrefetchScalarGridSpec(
            num_scalar_prefetch=1,
            grid=(nblk // BATCH,),
            in_specs=[
                pl.BlockSpec((BATCH, 1, half, width), lambda i, core: (i, core[0], 0, 0)),
                pl.BlockSpec((BATCH, half, width), lambda i, core: (i, 0, 0)),
            ],
            out_specs=pl.BlockSpec((NX, BATCH, half, quarter), lambda i, core: (0, i, 0, 0)),
        ),
        out_shape=bf16(NX, nblk, half, quarter),
        compiler_params=LIMIT,
    )(core.astype(jnp.int32)[None], halves, come)
    along_x = lax.all_to_all(pairs, "x", 0, 0, tiled=True)
    one = (shift(own, 1), shift(own, -1))
    along_x, one = lax.optimization_barrier((along_x, one))
    routed = kernel_call(
        route_kernel,
        bf16(slot_blocks.shape[0], half, quarter),
        [pltpu.VMEM((nblk, half, quarter), BF16)],
        (slot_blocks[:, 0],),
        along_x,
    )
    live = jnp.stack([counts[0], lax.axis_index("mp").astype(jnp.int32)])
    routed, live = lax.optimization_barrier((routed, live))
    owned = lax.all_to_all(routed, DP, 0, 0, tiled=True)
    two = (shift(one[0], 1), shift(one[1], -1))
    three = (shift(two[0], 1), shift(two[1], -1))
    owned, three = lax.optimization_barrier((owned, three))
    copies = kernel_call(collect_kernel, bf16(n_mp, rows, width), [], (), owned)
    g = lax.all_to_all(copies, "mp", 0, 0, tiled=True)
    four = shift(three[0], 1)
    roots = (own, *one, *two, *three, four)
    shape = bf16(rows, width)
    outs = kernel_call(
        finish_kernel,
        (shape, shape, shape),
        [pltpu.VMEM((width, width), BF16), pltpu.VMEM((width, width), F32)] + [pltpu.VMEM((width, width), BF16)] * 2,
        (live,),
        g,
        left_stat[0, 0],
        right_stat[0, 0],
        *roots,
    )
    return tuple(o[None, None] for o in outs)


def solution(mesh):
    fine = Mesh(mesh.devices.reshape(NZ, NX, NC, mesh.devices.shape[1]), ("z", "x", "c", "mp"))
    rows = P(DP, None, "mp", None)
    return jax.shard_map(
        on_device,
        mesh=fine,
        in_specs=(rows, P(), P(DP), rows, rows, rows, P(DP, None, None, "mp")),
        out_specs=(rows, rows, rows),
        check_vma=False,
    )
```

time: 110 us -> 89.9 us (0.82)
  starting transfers between devices: 18.1 us -> 52.4 us
  blocking collectives: 22.7 us -> 0 us
  waiting for transfers between devices: 43.3 us -> 26.9 us
  between operations: 14.8 us -> 1.39 us
  other arithmetic: 2.23 us -> 0.09 us
  Pallas kernels: 5.29 us -> 7 us
  local copies, waits for them, and re-layouts: 2.71 us -> 1.47 us
    ppermute x0 -> x7, starting transfers between devices: none -> 25.3 us  [shift(): return lax.ppermute(a, 'mp', [(i, (i + k) % n_mp) for i in range(n_mp)])]
    all_gather x1 -> x0, waiting for transfers between devices: 23.7 us -> none  [on_device(): roots_all = lax.all_gather(roots, 'mp', axis=0)]
    all_to_all x1 -> x0, blocking collectives: 22.7 us -> none  [on_device(): along_x = lax.all_to_all(pair, 'x', 0, 0, tiled=True)]
    ppermute x0 -> x7, waiting for transfers between devices: none -> 17.7 us  [shift(): return lax.ppermute(a, 'mp', [(i, (i + k) % n_mp) for i in range(n_mp)])]
    all_to_all x1, waiting for transfers between devices: 16.8 us -> 0.01 us  [on_device(): owned = lax.all_to_all(routed, DP, 0, 0, tiled=True)]
    all_to_all x1 -> x2, starting transfers between devices: 7.1 us -> 17.1 us  [the longest x1 9.52 us: on_device(): along_x = lax.all_to_all(pairs, 'x', 0, 0, tiled=True)]
    all_to_all x1 -> x2, waiting for transfers between devices: 0.01 us -> 6.66 us  [the longest x1 4.63 us: on_device(): along_x = lax.all_to_all(pairs, 'x', 0, 0, tiled=True)]
    pallas_call x3 -> x4, Pallas kernels: 5.29 us -> 7 us  [the longest x3 5.25 us: kernel_call(): pl.pallas_call(kernel, out_shape=out_shape, in_specs=[SMEM] * len(scalars...]
  transfers between devices with their start and end apart: 4 -> 11, of which waited for: 3 -> 9; matrix products, arithmetic and copies ran while one was open for 1% -> 0% of each run, Pallas kernels for 1% -> 0%
where the time goes in v2:
time: 89.9 us; the launch traced here: 89.3 us
  starting transfers between devices  52.4 us (58%)
  waiting for transfers between devices  26.9 us (30%)
  Pallas kernels  7 us (8%)
  local copies, waits for them, and re-layouts  1.47 us (2%)
  between operations  1.39 us (2%)
    ppermute x7, starting transfers between devices, shift(): return lax.ppermute(a, 'mp', [(i, (i + k) % n_mp) for i in range(n_mp)])  25.3 us
    ppermute x7, waiting for transfers between devices, shift(): return lax.ppermute(a, 'mp', [(i, (i + k) % n_mp) for i in range(n_mp)])  17.7 us
    all_to_all x1, starting transfers between devices, on_device(): along_x = lax.all_to_all(pairs, 'x', 0, 0, tiled=True)  9.52 us
    all_to_all x1, starting transfers between devices, on_device(): owned = lax.all_to_all(routed, DP, 0, 0, tiled=True)  8.09 us
    all_to_all x1, starting transfers between devices, on_device(): g = lax.all_to_all(copies, 'mp', 0, 0, tiled=True)  7.56 us
    pallas_call x3, Pallas kernels, kernel_call(): pl.pallas_call(kernel, out_shape=out_shape, in_specs=[SMEM] * len(scalars...  5.25 us
    all_to_all x1, waiting for transfers between devices, on_device(): along_x = lax.all_to_all(pairs, 'x', 0, 0, tiled=True)  4.63 us
    ppermute x1, waiting for transfers between devices, on_device(): come = lax.ppermute(away, 'c', [(0, 1), (1, 0)])  2.63 us
  transfers between devices with their start and end apart: 11, of which 9 were waited for; matrix products, arithmetic and copies ran while one was open for 0% of the time, Pallas kernels for 0%

profile of v2, /device:TPU:2, one launch (start us, length us, event | category | flops | bytes accessed | tf_op | source)
XLA Modules:
  0.0 89.3 jit_solution(12979758947499498375)
XLA Ops:
  0.6 0.0 copy-start
  0.6 1.4 %dynamic-slice_bitcast_fusion = bf16[32,32,512]{2,1,0:T(8,128)(2,1)S(1)} fusion(bf16[32,2,32,512]{3,2,1,0:T(8,128)(2,1)} %bitcast.17, s32[]{:T(128)S(6)} %select_n.4), kind=kLoop, calls=%fused_computation | loop fusion | bytes 2097156 | tf_op jit(solution)/shard_map/jit(dynamic_index_in_dim)/squeeze | solution.py:119
  2.1 1.9 %collective-permute-start = (bf16[32,32,512]{2,1,0:T(8,128)(2,1)S(1)}, bf16[32,32,512]{2,1,0:T(8,128)(2,1)S(1)}, u32[]{:S(2)}, u32[]{:S(2)}) collective-permute-start(bf16[32,32,512]{2,1,0:T(8,128)(2,1)S(1)} %dynamic-slice_bitcast_fusion), channel_id=1, source_target_pairs={{0,8},{8,0},{1,9},{9,1},{2,10},{10,2},{3,11},{11,3},{4,12},{12,4},... | collective-permute-start | bytes 3145736 | tf_op jit(solution)/shard_map/ppermute | solution.py:120
  4.0 2.6 %collective-permute-done.come_ref = bf16[32,32,512]{2,1,0:T(8,128)(2,1)S(1)} collective-permute-done((bf16[32,32,512]{2,1,0:T(8,128)(2,1)S(1)}, bf16[32,32,512]{2,1,0:T(8,128)(2,1)S(1)}, u32[]{:S(2)}, u32[]{:S(2)}) %collective-permute-start) | collective-permute-done | bytes 1048608 | tf_op jit(solution)/shard_map/ppermute | solution.py:120
  6.7 0.0 copy-done
  6.7 1.8 %shard_map.94 = bf16[4,32,32,128]{3,2,1,0:T(8,128)(2,1)} custom-call(s32[1]{0:T(128)} %bitcast.1.core_ref, bf16[32,2,32,512]{3,2,1,0:T(8,128)(2,1)S(1)} %bitcast.18, bf16[32,32,512]{2,1,0:T(8,128)(2,1)S(1)} %collective-permute-done.come_ref), custom_call_target="tpu_custom_call" | custom-call | tf_op jit(solution)/shard_map/pallas_call | solution.py:126
  8.4 0.0 copy-start.4
  8.4 0.0 copy-start.5
  8.4 0.0 copy-start.3
  8.4 9.5 %all-to-all-start = ((bf16[4,32,32,128]{3,2,1,0:T(8,128)(2,1)}), bf16[4,32,32,128]{3,2,1,0:T(8,128)(2,1)S(1)}, u32[]{:S(2)}, u32[]{:S(2)}) async-start(bf16[4,32,32,128]{3,2,1,0:T(8,128)(2,1)} %shard_map.94), calls=%async_computation | async-start | bytes 2097152 | tf_op jit(solution)/shard_map/all_to_all | solution.py:140
  17.9 0.0 copy-done.4
  17.9 0.0 copy-done.5
  18.0 1.9 %collective-permute-start.1 = (bf16[2,64,512]{2,1,0:T(8,128)(2,1)S(1)}, bf16[2,64,512]{2,1,0:T(8,128)(2,1)S(1)}, u32[]{:S(2)}, u32[]{:S(2)}) collective-permute-start(bf16[2,64,512]{2,1,0:T(8,128)(2,1)S(1)} %pad_maximum_fusion.refs_0_), channel_id=1, source_target_pairs={{0,1},{1,2},{2,3},{3,4},{4,5},{5,6},{6,7},{7,0},{8,9},{9,10},{10,1... | collective-permute-start | bytes 393224 | tf_op jit(solution)/shard_map/ppermute | solution.py:123
  19.9 5.1 %collective-permute-start.2 = (bf16[2,64,512]{2,1,0:T(8,128)(2,1)S(1)}, bf16[2,64,512]{2,1,0:T(8,128)(2,1)S(1)}, u32[]{:S(2)}, u32[]{:S(2)}) collective-permute-start(bf16[2,64,512]{2,1,0:T(8,128)(2,1)S(1)} %pad_maximum_fusion.refs_0_), channel_id=1, source_target_pairs={{0,7},{1,0},{2,1},{3,2},{4,3},{5,4},{6,5},{7,6},{8,15},{9,8},{10,9... | collective-permute-start | bytes 393224 | tf_op jit(solution)/shard_map/ppermute | solution.py:123
  25.7 0.1 pad_add_fusion.live_ref
  25.8 0.6 collective-permute-done.1.refs_1_
  26.3 1.2 %collective-permute-done.2.refs_2_ = bf16[2,64,512]{2,1,0:T(8,128)(2,1)S(1)} collective-permute-done((bf16[2,64,512]{2,1,0:T(8,128)(2,1)S(1)}, bf16[2,64,512]{2,1,0:T(8,128)(2,1)S(1)}, u32[]{:S(2)}, u32[]{:S(2)}) %collective-permute-start.2) | collective-permute-done | bytes 131104 | tf_op jit(solution)/shard_map/ppermute | solution.py:123
  27.5 4.6 %all-to-all-done.terms_ref = bf16[4,32,32,128]{3,2,1,0:T(8,128)(2,1)S(1)} async-done(((bf16[4,32,32,128]{3,2,1,0:T(8,128)(2,1)}), bf16[4,32,32,128]{3,2,1,0:T(8,128)(2,1)S(1)}, u32[]{:S(2)}, u32[]{:S(2)}) %all-to-all-start) | async-done | bytes 1048608 | tf_op jit(solution)/shard_map/all_to_all | solution.py:140
  32.2 0.0 copy-done.3
  32.2 0.0 copy-start.1
  32.2 0.0 copy-start.2
  32.2 1.7 %shard_map.95 = bf16[64,32,128]{2,1,0:T(8,128)(2,1)} custom-call(s32[64]{0:T(128)S(1)} %bitcast.21, bf16[4,32,32,128]{3,2,1,0:T(8,128)(2,1)S(1)} %all-to-all-done.terms_ref), custom_call_target="tpu_custom_call" | custom-call | tf_op jit(solution)/shard_map/pallas_call | solution.py:97
  33.8 8.1 %all-to-all-start.1 = ((bf16[64,32,128]{2,1,0:T(8,128)(2,1)}), bf16[64,32,128]{2,1,0:T(8,128)(2,1)S(1)}, u32[]{:S(2)}, u32[]{:S(2)}) async-start(bf16[64,32,128]{2,1,0:T(8,128)(2,1)} %shard_map.95), calls=%async_computation.1 | async-start | bytes 1048576 | tf_op jit(solution)/shard_map/all_to_all | solution.py:152
  41.9 3.5 %collective-permute-start.3 = (bf16[2,64,512]{2,1,0:T(8,128)(2,1)S(1)}, bf16[2,64,512]{2,1,0:T(8,128)(2,1)S(1)}, u32[]{:S(2)}, u32[]{:S(2)}) collective-permute-start(bf16[2,64,512]{2,1,0:T(8,128)(2,1)S(1)} %collective-permute-done.1.refs_1_), channel_id=1, source_target_pairs={{0,1},{1,2},{2,3},{3,4},{4,5},{5,6},{6,7},{7,0},{8,9},{9,10},{10,1... | collective-permute-start | bytes 393224 | tf_op jit(solution)/shard_map/ppermute | solution.py:123
  45.4 3.8 %collective-permute-start.5 = (bf16[2,64,512]{2,1,0:T(8,128)(2,1)S(1)}, bf16[2,64,512]{2,1,0:T(8,128)(2,1)S(1)}, u32[]{:S(2)}, u32[]{:S(2)}) collective-permute-start(bf16[2,64,512]{2,1,0:T(8,128)(2,1)S(1)} %collective-permute-done.2.refs_2_), channel_id=1, source_target_pairs={{0,7},{1,0},{2,1},{3,2},{4,3},{5,4},{6,5},{7,6},{8,15},{9,8},{10,9... | collective-permute-start | bytes 393224 | tf_op jit(solution)/shard_map/ppermute | solution.py:123
  49.2 1.9 %collective-permute-done.3.refs_3_ = bf16[2,64,512]{2,1,0:T(8,128)(2,1)S(1)} collective-permute-done((bf16[2,64,512]{2,1,0:T(8,128)(2,1)S(1)}, bf16[2,64,512]{2,1,0:T(8,128)(2,1)S(1)}, u32[]{:S(2)}, u32[]{:S(2)}) %collective-permute-start.3) | collective-permute-done | bytes 131104 | tf_op jit(solution)/shard_map/ppermute | solution.py:123
  51.1 1.9 %collective-permute-start.4 = (bf16[2,64,512]{2,1,0:T(8,128)(2,1)S(1)}, bf16[2,64,512]{2,1,0:T(8,128)(2,1)S(1)}, u32[]{:S(2)}, u32[]{:S(2)}) collective-permute-start(bf16[2,64,512]{2,1,0:T(8,128)(2,1)S(1)} %collective-permute-done.3.refs_3_), channel_id=1, source_target_pairs={{0,1},{1,2},{2,3},{3,4},{4,5},{5,6},{6,7},{7,0},{8,9},{9,10},{10,1... | collective-permute-start | bytes 393224 | tf_op jit(solution)/shard_map/ppermute | solution.py:123
  53.0 0.0 collective-permute-done.5.refs_4_
  53.0 5.1 %collective-permute-start.6 = (bf16[2,64,512]{2,1,0:T(8,128)(2,1)S(1)}, bf16[2,64,512]{2,1,0:T(8,128)(2,1)S(1)}, u32[]{:S(2)}, u32[]{:S(2)}) collective-permute-start(bf16[2,64,512]{2,1,0:T(8,128)(2,1)S(1)} %collective-permute-done.5.refs_4_), channel_id=1, source_target_pairs={{0,7},{1,0},{2,1},{3,2},{4,3},{5,4},{6,5},{7,6},{8,15},{9,8},{10,9... | collective-permute-start | bytes 393224 | tf_op jit(solution)/shard_map/ppermute | solution.py:123
  58.2 1.1 %collective-permute-done.4.refs_5_ = bf16[2,64,512]{2,1,0:T(8,128)(2,1)S(1)} collective-permute-done((bf16[2,64,512]{2,1,0:T(8,128)(2,1)S(1)}, bf16[2,64,512]{2,1,0:T(8,128)(2,1)S(1)}, u32[]{:S(2)}, u32[]{:S(2)}) %collective-permute-start.4) | collective-permute-done | bytes 131104 | tf_op jit(solution)/shard_map/ppermute | solution.py:123
  59.2 1.4 %collective-permute-done.6.refs_6_ = bf16[2,64,512]{2,1,0:T(8,128)(2,1)S(1)} collective-permute-done((bf16[2,64,512]{2,1,0:T(8,128)(2,1)S(1)}, bf16[2,64,512]{2,1,0:T(8,128)(2,1)S(1)}, u32[]{:S(2)}, u32[]{:S(2)}) %collective-permute-start.6) | collective-permute-done | bytes 131104 | tf_op jit(solution)/shard_map/ppermute | solution.py:123
  60.7 0.0 all-to-all-done.1.terms_ref
  60.7 0.9 shard_map.96
  61.6 7.6 %all-to-all-start.2 = ((bf16[8,64,512]{2,1,0:T(8,128)(2,1)}), bf16[8,64,512]{2,1,0:T(8,128)(2,1)S(1)}, u32[]{:S(2)}, u32[]{:S(2)}) async-start(bf16[8,64,512]{2,1,0:T(8,128)(2,1)} %shard_map.96), calls=%async_computation.2 | async-start | bytes 1048576 | tf_op jit(solution)/shard_map/all_to_all | solution.py:157
  69.1 3.9 %collective-permute-start.7 = (bf16[2,64,512]{2,1,0:T(8,128)(2,1)S(1)}, bf16[2,64,512]{2,1,0:T(8,128)(2,1)S(1)}, u32[]{:S(2)}, u32[]{:S(2)}) collective-permute-start(bf16[2,64,512]{2,1,0:T(8,128)(2,1)S(1)} %collective-permute-done.4.refs_5_), channel_id=1, source_target_pairs={{0,1},{1,2},{2,3},{3,4},{4,5},{5,6},{6,7},{7,0},{8,9},{9,10},{10,1... | collective-permute-start | bytes 393224 | tf_op jit(solution)/shard_map/ppermute | solution.py:123
  73.0 11.5 %collective-permute-done.7.refs_7_ = bf16[2,64,512]{2,1,0:T(8,128)(2,1)S(1)} collective-permute-done((bf16[2,64,512]{2,1,0:T(8,128)(2,1)S(1)}, bf16[2,64,512]{2,1,0:T(8,128)(2,1)S(1)}, u32[]{:S(2)}, u32[]{:S(2)}) %collective-permute-start.7) | collective-permute-done | bytes 131104 | tf_op jit(solution)/shard_map/ppermute | solution.py:123
  84.6 2.0 %all-to-all-done.2.parts_ref = bf16[8,64,512]{2,1,0:T(8,128)(2,1)S(1)} async-done(((bf16[8,64,512]{2,1,0:T(8,128)(2,1)}), bf16[8,64,512]{2,1,0:T(8,128)(2,1)S(1)}, u32[]{:S(2)}, u32[]{:S(2)}) %all-to-all-start.2) | async-done | bytes 524320 | tf_op jit(solution)/shard_map/all_to_all | solution.py:157
  86.6 0.0 copy-done.1
  86.6 0.0 copy-done.2
  86.6 2.7 %shard_map.97 = (bf16[64,512]{1,0:T(8,128)(2,1)}, bf16[64,512]{1,0:T(8,128)(2,1)}, bf16[64,512]{1,0:T(8,128)(2,1)}) custom-call(s32[2]{0:T(128)S(1)} %pad_add_fusion.live_ref, bf16[8,64,512]{2,1,0:T(8,128)(2,1)S(1)} %all-to-all-done.2.parts_ref, bf16[64,512]{1,0:T(8,128)(2,1)S(1)} %bitcast.19, bf16[64,512]{1,0:T(8,128)(2,1)S(1)} %bitcast.20, ...), custom_call_target="tpu_custom_call" | custom-call | tf_op jit(solution)/shard_map/pallas_call | solution.py:97
  (1 shorter events, 0.0 us)
Async XLA Ops:
  0.6 6.0 %copy-start = (bf16[1,32,64,512]{3,2,1,0:T(8,128)(2,1)S(1)}, bf16[1,32,64,512]{3,2,1,0:T(8,128)(2,1)}, u32[]{:S(2)}) copy-start(bf16[1,32,64,512]{3,2,1,0:T(8,128)(2,1)} %param.7) | copy-start | bytes 6291460
  2.1 4.6 %collective-permute-start = (bf16[32,32,512]{2,1,0:T(8,128)(2,1)S(1)}, bf16[32,32,512]{2,1,0:T(8,128)(2,1)S(1)}, u32[]{:S(2)}, u32[]{:S(2)}) collective-permute-start(bf16[32,32,512]{2,1,0:T(8,128)(2,1)S(1)} %dynamic-slice_bitcast_fusion), channel_id=1, source_target_pairs={{0,8},{8,0},{1,9},{9,1},{2,10},{10,2},{3,11},{11,3},{4,12},{12,4},... | collective-permute-start | bytes 3145736 | tf_op jit(solution)/shard_map/ppermute | solution.py:120
  8.4 9.5 %copy-start.4 = (bf16[1,1,512,64]{2,3,1,0:T(8,128)(2,1)S(1)}, bf16[1,1,512,64]{2,3,1,0:T(8,128)(2,1)}, u32[]{:S(2)}) copy-start(bf16[1,1,512,64]{2,3,1,0:T(8,128)(2,1)} %param.13) | copy-start | bytes 196612
  8.4 9.5 %copy-start.5 = (bf16[1,1,64,512]{3,2,1,0:T(8,128)(2,1)S(1)}, bf16[1,1,64,512]{3,2,1,0:T(8,128)(2,1)}, u32[]{:S(2)}) copy-start(bf16[1,1,64,512]{3,2,1,0:T(8,128)(2,1)} %param.12) | copy-start | bytes 196612
  8.4 23.7 %copy-start.3 = (s32[64,1]{0,1:T(1,128)S(1)}, s32[64,1]{0,1:T(1,128)}, u32[]{:S(2)}) copy-start(s32[64,1]{0,1:T(1,128)} %param.8) | copy-start | bytes 772
  8.4 23.7 %all-to-all-start = ((bf16[4,32,32,128]{3,2,1,0:T(8,128)(2,1)}), bf16[4,32,32,128]{3,2,1,0:T(8,128)(2,1)S(1)}, u32[]{:S(2)}, u32[]{:S(2)}) async-start(bf16[4,32,32,128]{3,2,1,0:T(8,128)(2,1)} %shard_map.94), calls=%async_computation | async-start | bytes 2097152 | tf_op jit(solution)/shard_map/all_to_all | solution.py:140
  18.0 8.4 %collective-permute-start.1 = (bf16[2,64,512]{2,1,0:T(8,128)(2,1)S(1)}, bf16[2,64,512]{2,1,0:T(8,128)(2,1)S(1)}, u32[]{:S(2)}, u32[]{:S(2)}) collective-permute-start(bf16[2,64,512]{2,1,0:T(8,128)(2,1)S(1)} %pad_maximum_fusion.refs_0_), channel_id=1, source_target_pairs={{0,1},{1,2},{2,3},{3,4},{4,5},{5,6},{6,7},{7,0},{8,9},{9,10},{10,1... | collective-permute-start | bytes 393224 | tf_op jit(solution)/shard_map/ppermute | solution.py:123
  19.9 7.6 %collective-permute-start.2 = (bf16[2,64,512]{2,1,0:T(8,128)(2,1)S(1)}, bf16[2,64,512]{2,1,0:T(8,128)(2,1)S(1)}, u32[]{:S(2)}, u32[]{:S(2)}) collective-permute-start(bf16[2,64,512]{2,1,0:T(8,128)(2,1)S(1)} %pad_maximum_fusion.refs_0_), channel_id=1, source_target_pairs={{0,7},{1,0},{2,1},{3,2},{4,3},{5,4},{6,5},{7,6},{8,15},{9,8},{10,9... | collective-permute-start | bytes 393224 | tf_op jit(solution)/shard_map/ppermute | solution.py:123
  32.2 54.4 %copy-start.1 = (bf16[1,1,64,512]{3,2,1,0:T(8,128)(2,1)S(1)}, bf16[1,1,64,512]{3,2,1,0:T(8,128)(2,1)}, u32[]{:S(2)}) copy-start(bf16[1,1,64,512]{3,2,1,0:T(8,128)(2,1)} %param.10) | copy-start | bytes 196612
  32.2 54.4 %copy-start.2 = (bf16[1,1,64,512]{3,2,1,0:T(8,128)(2,1)S(1)}, bf16[1,1,64,512]{3,2,1,0:T(8,128)(2,1)}, u32[]{:S(2)}) copy-start(bf16[1,1,64,512]{3,2,1,0:T(8,128)(2,1)} %param.11) | copy-start | bytes 196612
  33.8 26.8 %all-to-all-start.1 = ((bf16[64,32,128]{2,1,0:T(8,128)(2,1)}), bf16[64,32,128]{2,1,0:T(8,128)(2,1)S(1)}, u32[]{:S(2)}, u32[]{:S(2)}) async-start(bf16[64,32,128]{2,1,0:T(8,128)(2,1)} %shard_map.95), calls=%async_computation.1 | async-start | bytes 1048576 | tf_op jit(solution)/shard_map/all_to_all | solution.py:152
  41.9 9.2 %collective-permute-start.3 = (bf16[2,64,512]{2,1,0:T(8,128)(2,1)S(1)}, bf16[2,64,512]{2,1,0:T(8,128)(2,1)S(1)}, u32[]{:S(2)}, u32[]{:S(2)}) collective-permute-start(bf16[2,64,512]{2,1,0:T(8,128)(2,1)S(1)} %collective-permute-done.1.refs_1_), channel_id=1, source_target_pairs={{0,1},{1,2},{2,3},{3,4},{4,5},{5,6},{6,7},{7,0},{8,9},{9,10},{10,1... | collective-permute-start | bytes 393224 | tf_op jit(solution)/shard_map/ppermute | solution.py:123
  45.4 7.6 %collective-permute-start.5 = (bf16[2,64,512]{2,1,0:T(8,128)(2,1)S(1)}, bf16[2,64,512]{2,1,0:T(8,128)(2,1)S(1)}, u32[]{:S(2)}, u32[]{:S(2)}) collective-permute-start(bf16[2,64,512]{2,1,0:T(8,128)(2,1)S(1)} %collective-permute-done.2.refs_2_), channel_id=1, source_target_pairs={{0,7},{1,0},{2,1},{3,2},{4,3},{5,4},{6,5},{7,6},{8,15},{9,8},{10,9... | collective-permute-start | bytes 393224 | tf_op jit(solution)/shard_map/ppermute | solution.py:123
  51.1 8.1 %collective-permute-start.4 = (bf16[2,64,512]{2,1,0:T(8,128)(2,1)S(1)}, bf16[2,64,512]{2,1,0:T(8,128)(2,1)S(1)}, u32[]{:S(2)}, u32[]{:S(2)}) collective-permute-start(bf16[2,64,512]{2,1,0:T(8,128)(2,1)S(1)} %collective-permute-done.3.refs_3_), channel_id=1, source_target_pairs={{0,1},{1,2},{2,3},{3,4},{4,5},{5,6},{6,7},{7,0},{8,9},{9,10},{10,1... | collective-permute-start | bytes 393224 | tf_op jit(solution)/shard_map/ppermute | solution.py:123
  53.0 7.6 %collective-permute-start.6 = (bf16[2,64,512]{2,1,0:T(8,128)(2,1)S(1)}, bf16[2,64,512]{2,1,0:T(8,128)(2,1)S(1)}, u32[]{:S(2)}, u32[]{:S(2)}) collective-permute-start(bf16[2,64,512]{2,1,0:T(8,128)(2,1)S(1)} %collective-permute-done.5.refs_4_), channel_id=1, source_target_pairs={{0,7},{1,0},{2,1},{3,2},{4,3},{5,4},{6,5},{7,6},{8,15},{9,8},{10,9... | collective-permute-start | bytes 393224 | tf_op jit(solution)/shard_map/ppermute | solution.py:123
  61.6 25.0 %all-to-all-start.2 = ((bf16[8,64,512]{2,1,0:T(8,128)(2,1)}), bf16[8,64,512]{2,1,0:T(8,128)(2,1)S(1)}, u32[]{:S(2)}, u32[]{:S(2)}) async-start(bf16[8,64,512]{2,1,0:T(8,128)(2,1)} %shard_map.96), calls=%async_computation.2 | async-start | bytes 1048576 | tf_op jit(solution)/shard_map/all_to_all | solution.py:157
  69.1 15.4 %collective-permute-start.7 = (bf16[2,64,512]{2,1,0:T(8,128)(2,1)S(1)}, bf16[2,64,512]{2,1,0:T(8,128)(2,1)S(1)}, u32[]{:S(2)}, u32[]{:S(2)}) collective-permute-start(bf16[2,64,512]{2,1,0:T(8,128)(2,1)S(1)} %collective-permute-done.4.refs_5_), channel_id=1, source_target_pairs={{0,1},{1,2},{2,3},{3,4},{4,5},{5,6},{6,7},{7,0},{8,9},{9,10},{10,1... | collective-permute-start | bytes 393224 | tf_op jit(solution)/shard_map/ppermute | solution.py:123

commit v3 on v2

v3 whole, which is shorter than its diff:
```python
import jax
import jax.numpy as jnp
from jax import lax
from jax.experimental import pallas as pl
from jax.experimental.pallas import tpu as pltpu
from jax.sharding import Mesh
from jax.sharding import PartitionSpec as P

BETA = 0.9
RATE = 0.5
EPS = 1e-06
NH, NL, NX, NC = 4, 2, 4, 2
F32 = jnp.float32
BF16 = jnp.bfloat16
BATCH = 16
SLOTS = 32
DP = ("zh", "zl", "x", "c")
BACK = ((0,), (4,), (1,), (7,), (5, 2), (3, 6))


def away_kernel(core_ref, terms_ref, out_ref, sem):
    copy = pltpu.make_async_copy(terms_ref.at[:, 1 - core_ref[0]], out_ref, sem)
    copy.start()
    copy.wait()


def pair_kernel(core_ref, terms_ref, come_ref, out_ref):
    batch = pl.ds(pl.program_id(0) * BATCH, BATCH)
    total = (terms_ref[batch, core_ref[0]].astype(F32) + come_ref[batch].astype(F32)).astype(BF16)
    rows = out_ref.shape[2]
    for z in range(NL):
        for x in range(NX):
            out_ref[z * NX + x] = total[:, z * rows : (z + 1) * rows, x * 128 : (x + 1) * 128]


def route_kernel(ids_ref, terms_ref, out_ref, held_ref):
    nblk = held_ref.shape[0]
    first = pl.program_id(0) * out_ref.shape[0]

    @pl.when(first == 0)
    def _():
        total = terms_ref[0].astype(F32)
        for i in range(1, NL * NX):
            total += terms_ref[i].astype(F32)
        held_ref[...] = total.astype(BF16)

    for k in range(out_ref.shape[0]):
        b = jnp.clip(ids_ref[first + k], 0, nblk - 1)
        out_ref[k] = held_ref[b]


def collect_kernel(terms_ref, out_ref):
    n_out, rows = out_ref.shape[0], terms_ref.shape[1]
    parts = NL * NX * NC
    for z in range(NL):
        for x in range(NX):
            for c in range(NC):
                part = (z * NX + x) * NC + c
                total = terms_ref[part].astype(F32)
                for h in range(1, NH):
                    total += terms_ref[h * parts + part].astype(F32)
                low = total.astype(BF16)
                for k in range(n_out):
                    out_ref[k, pl.ds((c * NL + z) * rows, rows), pl.ds(x * 128, 128)] = low


def finish_kernel(live_ref, parts_ref, lstat_ref, rstat_ref, *refs):
    n_mp, rows, width = parts_ref.shape
    root_refs, refs = refs[: len(BACK)], refs[len(BACK) :]
    left_ref, right_ref, update_ref, gram_ref, lroot_ref, rroot_ref = refs
    m = live_ref[1]
    alive = live_ref[0] > 0
    g = parts_ref[...].reshape(width, width)
    cells = float(width * width)
    nt = (((1,), (1,)), ((), ()))
    tn = (((0,), (0,)), ((), ()))
    gram_left = lax.dot_general(parts_ref[m], g, nt, preferred_element_type=F32)
    lstat, rstat = lstat_ref[...], rstat_ref[...]
    new_left = (BETA * lstat.astype(F32) + (1.0 - BETA) * gram_left).astype(BF16)
    left_ref[...] = jnp.where(alive, new_left, lstat)
    cols = parts_ref[:, :, pl.ds(pl.multiple_of(lax.div(m, 2) * 128, 128), 128)].reshape(width, 128)
    gram_ref[...] = lax.dot_general(cols, g, tn, preferred_element_type=F32)
    gram_right = gram_ref[pl.ds(pl.multiple_of(lax.rem(m, 2) * rows, rows), rows), :]
    new_right = (BETA * rstat.astype(F32) + (1.0 - BETA) * gram_right).astype(BF16)
    right_ref[...] = jnp.where(alive, new_right, rstat)
    blocks = [(ref.at[k], back) for ref, backs in zip(root_refs, BACK) for k, back in enumerate(backs)]
    for i, (ref, back) in enumerate(blocks):
        lroot_ref[pl.ds(i * rows, rows), :] = ref[0]
        place = lax.rem(m + n_mp - back, n_mp) * rows
        rroot_ref[pl.ds(pl.multiple_of(place, rows), rows), :] = ref[1]
    middle = lax.dot_general(g, rroot_ref[...], nt, preferred_element_type=F32).astype(BF16)
    pre = jnp.dot(lroot_ref[...], middle, preferred_element_type=F32)
    g_float = g.astype(F32)
    squares = jnp.sum(g_float * g_float)
    pre_squares = jnp.sum(pre * pre)
    top = jnp.full((1, 1), squares, F32) / cells
    bottom = jnp.full((1, 1), pre_squares, F32) / cells + EPS
    scale = jnp.sqrt(top) / jnp.sqrt(bottom)
    new_update = (-RATE * scale * pre[:rows]).astype(BF16)
    update_ref[...] = jnp.where(alive, new_update, jnp.zeros_like(new_update))


VMEM = pl.BlockSpec(memory_space=pltpu.VMEM)
SMEM = pl.BlockSpec(memory_space=pltpu.SMEM)
LIMIT = pltpu.CompilerParams(vmem_limit_bytes=16 * 1024 * 1024)


def kernel_call(kernel, out_shape, scratch, scalars, *arrays):
    return pl.pallas_call(
        kernel,
        out_shape=out_shape,
        in_specs=[SMEM] * len(scalars) + [VMEM] * len(arrays),
        out_specs=jax.tree.map(lambda _: VMEM, out_shape),
        scratch_shapes=scratch,
        compiler_params=LIMIT,
    )(*scalars, *arrays)


def bf16(*shape):
    return jax.ShapeDtypeStruct(shape, BF16)


def on_device(grads, slot_blocks, counts, left_stat, right_stat, left_root, right_root):
    terms = grads[0]
    nblk, rows, width = terms.shape
    n_mp = width // rows
    core = lax.axis_index("c")

    half, piece, quarter = rows // NC, rows // (NC * NL), width // NX
    halves = terms.reshape(nblk, NC, half, width)
    away = pl.pallas_call(
        away_kernel,
        out_shape=bf16(nblk, half, width),
        in_specs=[SMEM, pl.BlockSpec(memory_space=pltpu.HBM)],
        out_specs=VMEM,
        scratch_shapes=[pltpu.SemaphoreType.DMA],
        compiler_params=LIMIT,
    )(core.astype(jnp.int32)[None], halves)
    come = lax.ppermute(away, "c", [(0, 1), (1, 0)])

    def shift(a, k):
        return lax.ppermute(a, "mp", [(i, (i + k) % n_mp) for i in range(n_mp)])

    own = jnp.stack([left_root[0, 0], right_root[0, 0].T])[None]
    pairs = pl.pallas_call(
        pair_kernel,
        grid=(nblk // BATCH,),
        out_shape=bf16(NL * NX, nblk, piece, quarter),
        in_specs=[SMEM, VMEM, VMEM],
        out_specs=pl.BlockSpec((NL * NX, BATCH, piece, quarter), lambda i: (0, i, 0, 0)),
        compiler_params=LIMIT,
    )(core.astype(jnp.int32)[None], halves, come)
    along_x = lax.all_to_all(pairs, ("zl", "x"), 0, 0, tiled=True)
    four, one, seven = shift(own, 4), shift(own, 1), shift(own, -1)
    along_x, four, one, seven = lax.optimization_barrier((along_x, four, one, seven))
    owners = slot_blocks.shape[0]
    routed = pl.pallas_call(
        route_kernel,
        grid=(owners // SLOTS,),
        out_shape=bf16(owners, piece, quarter),
        in_specs=[SMEM, VMEM],
        out_specs=pl.BlockSpec((SLOTS, piece, quarter), lambda i: (i, 0, 0)),
        scratch_shapes=[pltpu.VMEM((nblk, piece, quarter), BF16)],
        compiler_params=LIMIT,
    )(slot_blocks[:, 0], along_x)
    live = jnp.stack([counts[0], lax.axis_index("mp").astype(jnp.int32)])
    routed, live = lax.optimization_barrier((routed, live))
    owned = lax.all_to_all(routed, DP, 0, 0, tiled=True)
    up = shift(jnp.concatenate([four, one]), 1)
    down = shift(jnp.concatenate([four, seven]), -1)
    owned, up, down = lax.optimization_barrier((owned, up, down))
    copies = kernel_call(collect_kernel, bf16(n_mp, rows, width), [], (), owned)
    g = lax.all_to_all(copies, "mp", 0, 0, tiled=True)
    roots = (own, four, one, seven, up, down)
    shape = bf16(rows, width)
    outs = kernel_call(
        finish_kernel,
        (shape, shape, shape),
        [pltpu.VMEM((128, width), F32)] + [pltpu.VMEM((width, width), BF16)] * 2,
        (live,),
        g,
        left_stat[0, 0],
        right_stat[0, 0],
        *roots,
    )
    return tuple(o[None, None] for o in outs)


def solution(mesh):
    fine = Mesh(mesh.devices.reshape(NH, NL, NX, NC, mesh.devices.shape[1]), (*DP, "mp"))
    rows = P(DP, None, "mp", None)
    return jax.shard_map(
        on_device,
        mesh=fine,
        in_specs=(rows, P(), P(DP), rows, rows, rows, P(DP, None, None, "mp")),
        out_specs=(rows, rows, rows),
        check_vma=False,
    )
```

time: 89.9 us -> 84.9 us (0.944)
  blocking collectives: 0 us -> 21.7 us
  waiting for transfers between devices: 26.9 us -> 10.7 us
  starting transfers between devices: 52.4 us -> 43.5 us
  Pallas kernels: 7 us -> 5.38 us
    all_to_all x0 -> x1, blocking collectives: none -> 21.7 us  [on_device(): g = lax.all_to_all(copies, 'mp', 0, 0, tiled=True)]
    ppermute x7 -> x5, waiting for transfers between devices: 17.7 us -> 8.04 us  [shift(): return lax.ppermute(a, 'mp', [(i, (i + k) % n_mp) for i in range(n_mp)])]
    all_to_all x2 -> x1, starting transfers between devices: 17.1 us -> 9.5 us  [on_device(): along_x = lax.all_to_all(pairs, ('zl', 'x'), 0, 0, tiled=True)]
    all_to_all x2 -> x1, waiting for transfers between devices: 6.66 us -> 0.01 us  [on_device(): along_x = lax.all_to_all(pairs, ('zl', 'x'), 0, 0, tiled=True)]
    ppermute x7 -> x5, starting transfers between devices: 25.3 us -> 19.6 us  [shift(): return lax.ppermute(a, 'mp', [(i, (i + k) % n_mp) for i in range(n_mp)])]
    all_to_all x1, starting transfers between devices: 8.09 us -> 12.5 us  [on_device(): owned = lax.all_to_all(routed, DP, 0, 0, tiled=True)]
    pallas_call x3 -> x2, Pallas kernels: 5.25 us -> 2.64 us  [kernel_call(): pl.pallas_call(kernel, out_shape=out_shape, in_specs=[SMEM] * len(scalars...]
    unnamed x12, local copies, waits for them, and re-layouts: 0.02 us -> 1.61 us
  transfers between devices with their start and end apart: 11 -> 8, of which waited for: 9 -> 5; matrix products, arithmetic and copies ran while one was open for 0% -> 0% of each run, Pallas kernels for 0% -> 0%
where the time goes in v3:
time: 84.9 us; the launch traced here: 84.4 us
  starting transfers between devices  43.5 us (51%)
  blocking collectives  21.7 us (26%)
  waiting for transfers between devices  10.7 us (13%)
  Pallas kernels  5.38 us (6%)
  local copies, waits for them, and re-layouts  1.61 us (2%)
  between operations  1.41 us (2%)
    all_to_all x1, blocking collectives, on_device(): g = lax.all_to_all(copies, 'mp', 0, 0, tiled=True)  21.7 us
    ppermute x5, starting transfers between devices, shift(): return lax.ppermute(a, 'mp', [(i, (i + k) % n_mp) for i in range(n_mp)])  19.6 us
    all_to_all x1, starting transfers between devices, on_device(): owned = lax.all_to_all(routed, DP, 0, 0, tiled=True)  12.5 us
    all_to_all x1, starting transfers between devices, on_device(): along_x = lax.all_to_all(pairs, ('zl', 'x'), 0, 0, tiled=True)  9.5 us
    ppermute x5, waiting for transfers between devices, shift(): return lax.ppermute(a, 'mp', [(i, (i + k) % n_mp) for i in range(n_mp)])  8.04 us
    pallas_call x2, Pallas kernels, kernel_call(): pl.pallas_call(kernel, out_shape=out_shape, in_specs=[SMEM] * len(scalars...  2.64 us
    ppermute x1, waiting for transfers between devices, on_device(): come = lax.ppermute(away, 'c', [(0, 1), (1, 0)])  2.63 us
    ppermute x1, starting transfers between devices, on_device(): come = lax.ppermute(away, 'c', [(0, 1), (1, 0)])  1.92 us
  transfers between devices with their start and end apart: 8, of which 5 were waited for; matrix products, arithmetic and copies ran while one was open for 0% of the time, Pallas kernels for 0%

profile of v3, /device:TPU:2, one launch (start us, length us, event | category | flops | bytes accessed | tf_op | source)
XLA Modules:
  0.0 84.4 jit_solution(11332497893825864662)
XLA Ops:
  0.6 0.0 copy-start
  0.6 1.6 %copy-done = bf16[1,32,64,512]{3,2,1,0:T(8,128)(2,1)S(1)} copy-done((bf16[1,32,64,512]{3,2,1,0:T(8,128)(2,1)S(1)}, bf16[1,32,64,512]{3,2,1,0:T(8,128)(2,1)}, u32[]{:S(2)}) %copy-start) | copy-done | bytes 2097176
  2.2 0.1 shard_map.94
  2.4 1.9 %collective-permute-start = (bf16[32,32,512]{2,1,0:T(8,128)(2,1)S(1)}, bf16[32,32,512]{2,1,0:T(8,128)(2,1)S(1)}, u32[]{:S(2)}, u32[]{:S(2)}) collective-permute-start(bf16[32,32,512]{2,1,0:T(8,128)(2,1)S(1)} %shard_map.94), channel_id=1, source_target_pairs={{0,8},{8,0},{1,9},{9,1},{2,10},{10,2},{3,11},{11,3},{4,12},{12,4},... | collective-permute-start | bytes 3145736 | tf_op jit(solution)/shard_map/ppermute | solution.py:139
  4.3 2.6 %collective-permute-done.come_ref = bf16[32,32,512]{2,1,0:T(8,128)(2,1)S(1)} collective-permute-done((bf16[32,32,512]{2,1,0:T(8,128)(2,1)S(1)}, bf16[32,32,512]{2,1,0:T(8,128)(2,1)S(1)}, u32[]{:S(2)}, u32[]{:S(2)}) %collective-permute-start) | collective-permute-done | bytes 1048608 | tf_op jit(solution)/shard_map/ppermute | solution.py:139
  6.9 1.1 %shard_map.95 = bf16[8,32,16,128]{3,2,1,0:T(8,128)(2,1)} custom-call(s32[1]{0:T(128)} %bitcast.1.core_ref, bf16[32,2,32,512]{3,2,1,0:T(8,128)(2,1)S(1)} %bitcast.18, bf16[32,32,512]{2,1,0:T(8,128)(2,1)S(1)} %collective-permute-done.come_ref), custom_call_target="tpu_custom_call" | custom-call | tf_op jit(solution)/shard_map/pallas_call | solution.py:145
  8.0 0.0 copy-start.4
  8.0 0.0 copy-start.5
  8.0 0.0 copy-start.3
  8.0 9.5 %all-to-all-start = ((bf16[8,32,16,128]{3,2,1,0:T(8,128)(2,1)}), bf16[8,32,16,128]{3,2,1,0:T(8,128)(2,1)S(1)}, u32[]{:S(2)}, u32[]{:S(2)}) async-start(bf16[8,32,16,128]{3,2,1,0:T(8,128)(2,1)} %shard_map.95), calls=%async_computation | async-start | bytes 2097152 | tf_op jit(solution)/shard_map/all_to_all | solution.py:153
  17.5 0.0 copy-done.4
  17.5 0.0 copy-done.5
  17.6 5.0 %collective-permute-start.1 = (bf16[1,2,64,512]{3,2,1,0:T(8,128)(2,1)S(1)}, bf16[1,2,64,512]{3,2,1,0:T(8,128)(2,1)S(1)}, u32[]{:S(2)}, u32[]{:S(2)}) collective-permute-start(bf16[1,2,64,512]{3,2,1,0:T(8,128)(2,1)S(1)} %maximum_bitcast_fusion.refs_0_), channel_id=1, source_target_pairs={{0,4},{1,5},{2,6},{3,7},{4,0},{5,1},{6,2},{7,3},{8,12},{9,13},{10,... | collective-permute-start | bytes 393224 | tf_op jit(solution)/shard_map/ppermute | solution.py:142
  22.6 2.6 %collective-permute-start.2 = (bf16[1,2,64,512]{3,2,1,0:T(8,128)(2,1)S(1)}, bf16[1,2,64,512]{3,2,1,0:T(8,128)(2,1)S(1)}, u32[]{:S(2)}, u32[]{:S(2)}) collective-permute-start(bf16[1,2,64,512]{3,2,1,0:T(8,128)(2,1)S(1)} %maximum_bitcast_fusion.refs_0_), channel_id=1, source_target_pairs={{0,1},{1,2},{2,3},{3,4},{4,5},{5,6},{6,7},{7,0},{8,9},{9,10},{10,1... | collective-permute-start | bytes 393224 | tf_op jit(solution)/shard_map/ppermute | solution.py:142
  25.2 4.5 %collective-permute-start.3 = (bf16[1,2,64,512]{3,2,1,0:T(8,128)(2,1)S(1)}, bf16[1,2,64,512]{3,2,1,0:T(8,128)(2,1)S(1)}, u32[]{:S(2)}, u32[]{:S(2)}) collective-permute-start(bf16[1,2,64,512]{3,2,1,0:T(8,128)(2,1)S(1)} %maximum_bitcast_fusion.refs_0_), channel_id=1, source_target_pairs={{0,7},{1,0},{2,1},{3,2},{4,3},{5,4},{6,5},{7,6},{8,15},{9,8},{10,9... | collective-permute-start | bytes 393224 | tf_op jit(solution)/shard_map/ppermute | solution.py:142
  30.3 0.1 pad_add_fusion.live_ref
  30.4 1.9 %collective-permute-done.1.refs_1_ = bf16[1,2,64,512]{3,2,1,0:T(8,128)(2,1)S(1)} collective-permute-done((bf16[1,2,64,512]{3,2,1,0:T(8,128)(2,1)S(1)}, bf16[1,2,64,512]{3,2,1,0:T(8,128)(2,1)S(1)}, u32[]{:S(2)}, u32[]{:S(2)}) %collective-permute-start.1) | collective-permute-done | bytes 131104 | tf_op jit(solution)/shard_map/ppermute | solution.py:142
  32.2 0.3 collective-permute-done.2.refs_2_
  32.5 0.0 collective-permute-done.3.refs_3_
  32.5 0.0 all-to-all-done.terms_ref
  32.5 0.0 copy-done.3
  32.6 0.0 copy-start.1
  32.6 0.0 copy-start.2
  32.6 1.5 %shard_map.96 = bf16[64,16,128]{2,1,0:T(8,128)(2,1)} custom-call(s32[64]{0:T(128)S(1)} %bitcast.21, bf16[8,32,16,128]{3,2,1,0:T(8,128)(2,1)S(1)} %all-to-all-done.terms_ref), custom_call_target="tpu_custom_call" | custom-call | tf_op jit(solution)/shard_map/pallas_call | solution.py:157
  34.1 12.5 %all-to-all-start.1 = ((bf16[64,16,128]{2,1,0:T(8,128)(2,1)}), bf16[64,16,128]{2,1,0:T(8,128)(2,1)S(1)}, u32[]{:S(2)}, u32[]{:S(2)}) async-start(bf16[64,16,128]{2,1,0:T(8,128)(2,1)} %shard_map.96), calls=%async_computation.1 | async-start | bytes 524288 | tf_op jit(solution)/shard_map/all_to_all | solution.py:168
  46.7 2.9 %collective-permute-start.4 = (bf16[2,2,64,512]{3,2,1,0:T(8,128)(2,1)S(1)}, bf16[2,2,64,512]{3,2,1,0:T(8,128)(2,1)S(1)}, u32[]{:S(2)}, u32[]{:S(2)}) collective-permute-start(bf16[2,2,64,512]{3,2,1,0:T(8,128)(2,1)S(1)} %get-tuple-element.28), channel_id=1, source_target_pairs={{0,1},{1,2},{2,3},{3,4},{4,5},{5,6},{6,7},{7,0},{8,9},{9,10},{10,1... | collective-permute-start | bytes 786440 | tf_op jit(solution)/shard_map/ppermute | solution.py:142
  49.6 4.6 %collective-permute-start.5 = (bf16[2,2,64,512]{3,2,1,0:T(8,128)(2,1)S(1)}, bf16[2,2,64,512]{3,2,1,0:T(8,128)(2,1)S(1)}, u32[]{:S(2)}, u32[]{:S(2)}) collective-permute-start(bf16[2,2,64,512]{3,2,1,0:T(8,128)(2,1)S(1)} %get-tuple-element.27), channel_id=1, source_target_pairs={{0,7},{1,0},{2,1},{3,2},{4,3},{5,4},{6,5},{7,6},{8,15},{9,8},{10,9... | collective-permute-start | bytes 786440 | tf_op jit(solution)/shard_map/ppermute | solution.py:142
  54.2 4.7 %collective-permute-done.4.refs_4_ = bf16[2,2,64,512]{3,2,1,0:T(8,128)(2,1)S(1)} collective-permute-done((bf16[2,2,64,512]{3,2,1,0:T(8,128)(2,1)S(1)}, bf16[2,2,64,512]{3,2,1,0:T(8,128)(2,1)S(1)}, u32[]{:S(2)}, u32[]{:S(2)}) %collective-permute-start.4) | collective-permute-done | bytes 262176 | tf_op jit(solution)/shard_map/ppermute | solution.py:142
  58.8 1.2 %collective-permute-done.5.refs_5_ = bf16[2,2,64,512]{3,2,1,0:T(8,128)(2,1)S(1)} collective-permute-done((bf16[2,2,64,512]{3,2,1,0:T(8,128)(2,1)S(1)}, bf16[2,2,64,512]{3,2,1,0:T(8,128)(2,1)S(1)}, u32[]{:S(2)}, u32[]{:S(2)}) %collective-permute-start.5) | collective-permute-done | bytes 262176 | tf_op jit(solution)/shard_map/ppermute | solution.py:142
  60.0 0.0 all-to-all-done.1.terms_ref
  60.0 0.1 shard_map.97
  60.1 21.7 %all_to_all.15.parts_ref = bf16[8,64,512]{2,1,0:T(8,128)(2,1)S(1)} all-to-all(bf16[8,64,512]{2,1,0:T(8,128)(2,1)S(1)} %shard_map.97), channel_id=1, replica_groups=mesh['zh'=4,'zl'=2,'x'=4,'c'=2,'mp'=8] {'mp'}, dimensions={0} | all-to-all | bytes 1048576 | tf_op jit(solution)/shard_map/all_to_all | solution.py:173
  81.9 0.0 copy-done.1
  81.9 0.0 copy-done.2
  81.9 2.6 %shard_map.98 = (bf16[64,512]{1,0:T(8,128)(2,1)}, bf16[64,512]{1,0:T(8,128)(2,1)}, bf16[64,512]{1,0:T(8,128)(2,1)}) custom-call(s32[2]{0:T(128)S(1)} %pad_add_fusion.live_ref, bf16[8,64,512]{2,1,0:T(8,128)(2,1)S(1)} %all_to_all.15.parts_ref, bf16[64,512]{1,0:T(8,128)(2,1)S(1)} %bitcast.19, bf16[64,512]{1,0:T(8,128)(2,1)S(1)} %bitcast.20, ...), custom_call_target="tpu_custom_call" | custom-call | tf_op jit(solution)/shard_map/pallas_call | solution.py:109
  (2 shorter events, 0.1 us)
Async XLA Ops:
  0.6 1.6 %copy-start = (bf16[1,32,64,512]{3,2,1,0:T(8,128)(2,1)S(1)}, bf16[1,32,64,512]{3,2,1,0:T(8,128)(2,1)}, u32[]{:S(2)}) copy-start(bf16[1,32,64,512]{3,2,1,0:T(8,128)(2,1)} %param.7) | copy-start | bytes 6291460
  2.4 4.6 %collective-permute-start = (bf16[32,32,512]{2,1,0:T(8,128)(2,1)S(1)}, bf16[32,32,512]{2,1,0:T(8,128)(2,1)S(1)}, u32[]{:S(2)}, u32[]{:S(2)}) collective-permute-start(bf16[32,32,512]{2,1,0:T(8,128)(2,1)S(1)} %shard_map.94), channel_id=1, source_target_pairs={{0,8},{8,0},{1,9},{9,1},{2,10},{10,2},{3,11},{11,3},{4,12},{12,4},... | collective-permute-start | bytes 3145736 | tf_op jit(solution)/shard_map/ppermute | solution.py:139
  8.0 9.5 %copy-start.4 = (bf16[1,1,512,64]{2,3,1,0:T(8,128)(2,1)S(1)}, bf16[1,1,512,64]{2,3,1,0:T(8,128)(2,1)}, u32[]{:S(2)}) copy-start(bf16[1,1,512,64]{2,3,1,0:T(8,128)(2,1)} %param.13) | copy-start | bytes 196612
  8.0 9.5 %copy-start.5 = (bf16[1,1,64,512]{3,2,1,0:T(8,128)(2,1)S(1)}, bf16[1,1,64,512]{3,2,1,0:T(8,128)(2,1)}, u32[]{:S(2)}) copy-start(bf16[1,1,64,512]{3,2,1,0:T(8,128)(2,1)} %param.12) | copy-start | bytes 196612
  8.0 24.5 %copy-start.3 = (s32[64,1]{0,1:T(1,128)S(1)}, s32[64,1]{0,1:T(1,128)}, u32[]{:S(2)}) copy-start(s32[64,1]{0,1:T(1,128)} %param.8) | copy-start | bytes 772
  8.0 24.5 %all-to-all-start = ((bf16[8,32,16,128]{3,2,1,0:T(8,128)(2,1)}), bf16[8,32,16,128]{3,2,1,0:T(8,128)(2,1)S(1)}, u32[]{:S(2)}, u32[]{:S(2)}) async-start(bf16[8,32,16,128]{3,2,1,0:T(8,128)(2,1)} %shard_map.95), calls=%async_computation | async-start | bytes 2097152 | tf_op jit(solution)/shard_map/all_to_all | solution.py:153
  17.6 14.7 %collective-permute-start.1 = (bf16[1,2,64,512]{3,2,1,0:T(8,128)(2,1)S(1)}, bf16[1,2,64,512]{3,2,1,0:T(8,128)(2,1)S(1)}, u32[]{:S(2)}, u32[]{:S(2)}) collective-permute-start(bf16[1,2,64,512]{3,2,1,0:T(8,128)(2,1)S(1)} %maximum_bitcast_fusion.refs_0_), channel_id=1, source_target_pairs={{0,4},{1,5},{2,6},{3,7},{4,0},{5,1},{6,2},{7,3},{8,12},{9,13},{10,... | collective-permute-start | bytes 393224 | tf_op jit(solution)/shard_map/ppermute | solution.py:142
  22.6 10.0 %collective-permute-start.2 = (bf16[1,2,64,512]{3,2,1,0:T(8,128)(2,1)S(1)}, bf16[1,2,64,512]{3,2,1,0:T(8,128)(2,1)S(1)}, u32[]{:S(2)}, u32[]{:S(2)}) collective-permute-start(bf16[1,2,64,512]{3,2,1,0:T(8,128)(2,1)S(1)} %maximum_bitcast_fusion.refs_0_), channel_id=1, source_target_pairs={{0,1},{1,2},{2,3},{3,4},{4,5},{5,6},{6,7},{7,0},{8,9},{9,10},{10,1... | collective-permute-start | bytes 393224 | tf_op jit(solution)/shard_map/ppermute | solution.py:142
  25.2 7.4 %collective-permute-start.3 = (bf16[1,2,64,512]{3,2,1,0:T(8,128)(2,1)S(1)}, bf16[1,2,64,512]{3,2,1,0:T(8,128)(2,1)S(1)}, u32[]{:S(2)}, u32[]{:S(2)}) collective-permute-start(bf16[1,2,64,512]{3,2,1,0:T(8,128)(2,1)S(1)} %maximum_bitcast_fusion.refs_0_), channel_id=1, source_target_pairs={{0,7},{1,0},{2,1},{3,2},{4,3},{5,4},{6,5},{7,6},{8,15},{9,8},{10,9... | collective-permute-start | bytes 393224 | tf_op jit(solution)/shard_map/ppermute | solution.py:142
  32.6 49.3 %copy-start.1 = (bf16[1,1,64,512]{3,2,1,0:T(8,128)(2,1)S(1)}, bf16[1,1,64,512]{3,2,1,0:T(8,128)(2,1)}, u32[]{:S(2)}) copy-start(bf16[1,1,64,512]{3,2,1,0:T(8,128)(2,1)} %param.10) | copy-start | bytes 196612
  32.6 49.3 %copy-start.2 = (bf16[1,1,64,512]{3,2,1,0:T(8,128)(2,1)S(1)}, bf16[1,1,64,512]{3,2,1,0:T(8,128)(2,1)}, u32[]{:S(2)}) copy-start(bf16[1,1,64,512]{3,2,1,0:T(8,128)(2,1)} %param.11) | copy-start | bytes 196612
  34.1 25.9 %all-to-all-start.1 = ((bf16[64,16,128]{2,1,0:T(8,128)(2,1)}), bf16[64,16,128]{2,1,0:T(8,128)(2,1)S(1)}, u32[]{:S(2)}, u32[]{:S(2)}) async-start(bf16[64,16,128]{2,1,0:T(8,128)(2,1)} %shard_map.96), calls=%async_computation.1 | async-start | bytes 524288 | tf_op jit(solution)/shard_map/all_to_all | solution.py:168
  46.7 12.2 %collective-permute-start.4 = (bf16[2,2,64,512]{3,2,1,0:T(8,128)(2,1)S(1)}, bf16[2,2,64,512]{3,2,1,0:T(8,128)(2,1)S(1)}, u32[]{:S(2)}, u32[]{:S(2)}) collective-permute-start(bf16[2,2,64,512]{3,2,1,0:T(8,128)(2,1)S(1)} %get-tuple-element.28), channel_id=1, source_target_pairs={{0,1},{1,2},{2,3},{3,4},{4,5},{5,6},{6,7},{7,0},{8,9},{9,10},{10,1... | collective-permute-start | bytes 786440 | tf_op jit(solution)/shard_map/ppermute | solution.py:142
  49.6 10.4 %collective-permute-start.5 = (bf16[2,2,64,512]{3,2,1,0:T(8,128)(2,1)S(1)}, bf16[2,2,64,512]{3,2,1,0:T(8,128)(2,1)S(1)}, u32[]{:S(2)}, u32[]{:S(2)}) collective-permute-start(bf16[2,2,64,512]{3,2,1,0:T(8,128)(2,1)S(1)} %get-tuple-element.27), channel_id=1, source_target_pairs={{0,7},{1,0},{2,1},{3,2},{4,3},{5,4},{6,5},{7,6},{8,15},{9,8},{10,9... | collective-permute-start | bytes 786440 | tf_op jit(solution)/shard_map/ppermute | solution.py:142

commit v4 on v3

--- a/solution.py
+++ b/solution.py
@@ -12,8 +12,8 @@
 NH, NL, NX, NC = 4, 2, 4, 2
 F32 = jnp.float32
 BF16 = jnp.bfloat16
-BATCH = 16
-SLOTS = 32
+BATCH = 32
+SLOTS = 64
 DP = ("zh", "zl", "x", "c")
 BACK = ((0,), (4,), (1,), (7,), (5, 2), (3, 6))
 

time: 84.9 us -> 85 us (level)
  no operation moved by 1% of the time
where the time goes in v4:
time: 85 us; the launch traced here: 84.5 us
  starting transfers between devices  43.5 us (51%)
  blocking collectives  21.7 us (26%)
  waiting for transfers between devices  10.7 us (13%)
  Pallas kernels  5.5 us (6%)
  local copies, waits for them, and re-layouts  1.61 us (2%)
  between operations  1.41 us (2%)
    all_to_all x1, blocking collectives, on_device(): g = lax.all_to_all(copies, 'mp', 0, 0, tiled=True)  21.7 us
    ppermute x5, starting transfers between devices, shift(): return lax.ppermute(a, 'mp', [(i, (i + k) % n_mp) for i in range(n_mp)])  19.6 us
    all_to_all x1, starting transfers between devices, on_device(): owned = lax.all_to_all(routed, DP, 0, 0, tiled=True)  12.5 us
    all_to_all x1, starting transfers between devices, on_device(): along_x = lax.all_to_all(pairs, ('zl', 'x'), 0, 0, tiled=True)  9.5 us
    ppermute x5, waiting for transfers between devices, shift(): return lax.ppermute(a, 'mp', [(i, (i + k) % n_mp) for i in range(n_mp)])  8.04 us
    pallas_call x2, Pallas kernels, kernel_call(): pl.pallas_call(kernel, out_shape=out_shape, in_specs=[SMEM] * len(scalars...  2.64 us
    ppermute x1, waiting for transfers between devices, on_device(): come = lax.ppermute(away, 'c', [(0, 1), (1, 0)])  2.63 us
    ppermute x1, starting transfers between devices, on_device(): come = lax.ppermute(away, 'c', [(0, 1), (1, 0)])  1.92 us
  transfers between devices with their start and end apart: 8, of which 5 were waited for; matrix products, arithmetic and copies ran while one was open for 0% of the time, Pallas kernels for 0%

profile of v4, /device:TPU:2, one launch (start us, length us, event | category | flops | bytes accessed | tf_op | source)
XLA Modules:
  0.0 84.5 jit_solution(10987857240102601930)
XLA Ops:
  0.6 0.0 copy-start
  0.6 1.6 %copy-done = bf16[1,32,64,512]{3,2,1,0:T(8,128)(2,1)S(1)} copy-done((bf16[1,32,64,512]{3,2,1,0:T(8,128)(2,1)S(1)}, bf16[1,32,64,512]{3,2,1,0:T(8,128)(2,1)}, u32[]{:S(2)}) %copy-start) | copy-done | bytes 2097176
  2.2 0.1 shard_map.94
  2.4 1.9 %collective-permute-start = (bf16[32,32,512]{2,1,0:T(8,128)(2,1)S(1)}, bf16[32,32,512]{2,1,0:T(8,128)(2,1)S(1)}, u32[]{:S(2)}, u32[]{:S(2)}) collective-permute-start(bf16[32,32,512]{2,1,0:T(8,128)(2,1)S(1)} %shard_map.94), channel_id=1, source_target_pairs={{0,8},{8,0},{1,9},{9,1},{2,10},{10,2},{3,11},{11,3},{4,12},{12,4},... | collective-permute-start | bytes 3145736 | tf_op jit(solution)/shard_map/ppermute | solution.py:139
  4.3 2.6 %collective-permute-done.come_ref = bf16[32,32,512]{2,1,0:T(8,128)(2,1)S(1)} collective-permute-done((bf16[32,32,512]{2,1,0:T(8,128)(2,1)S(1)}, bf16[32,32,512]{2,1,0:T(8,128)(2,1)S(1)}, u32[]{:S(2)}, u32[]{:S(2)}) %collective-permute-start) | collective-permute-done | bytes 1048608 | tf_op jit(solution)/shard_map/ppermute | solution.py:139
  6.9 1.3 %shard_map.95 = bf16[8,32,16,128]{3,2,1,0:T(8,128)(2,1)} custom-call(s32[1]{0:T(128)} %bitcast.1.core_ref, bf16[32,2,32,512]{3,2,1,0:T(8,128)(2,1)S(1)} %bitcast.18, bf16[32,32,512]{2,1,0:T(8,128)(2,1)S(1)} %collective-permute-done.come_ref), custom_call_target="tpu_custom_call" | custom-call | tf_op jit(solution)/shard_map/pallas_call | solution.py:145
  8.2 0.0 copy-start.4
  8.2 0.0 copy-start.5
  8.2 0.0 copy-start.3
  8.2 9.5 %all-to-all-start = ((bf16[8,32,16,128]{3,2,1,0:T(8,128)(2,1)}), bf16[8,32,16,128]{3,2,1,0:T(8,128)(2,1)S(1)}, u32[]{:S(2)}, u32[]{:S(2)}) async-start(bf16[8,32,16,128]{3,2,1,0:T(8,128)(2,1)} %shard_map.95), calls=%async_computation | async-start | bytes 2097152 | tf_op jit(solution)/shard_map/all_to_all | solution.py:153
  17.7 0.0 copy-done.4
  17.7 0.0 copy-done.5
  17.7 5.0 %collective-permute-start.1 = (bf16[1,2,64,512]{3,2,1,0:T(8,128)(2,1)S(1)}, bf16[1,2,64,512]{3,2,1,0:T(8,128)(2,1)S(1)}, u32[]{:S(2)}, u32[]{:S(2)}) collective-permute-start(bf16[1,2,64,512]{3,2,1,0:T(8,128)(2,1)S(1)} %maximum_bitcast_fusion.refs_0_), channel_id=1, source_target_pairs={{0,4},{1,5},{2,6},{3,7},{4,0},{5,1},{6,2},{7,3},{8,12},{9,13},{10,... | collective-permute-start | bytes 393224 | tf_op jit(solution)/shard_map/ppermute | solution.py:142
  22.7 2.6 %collective-permute-start.2 = (bf16[1,2,64,512]{3,2,1,0:T(8,128)(2,1)S(1)}, bf16[1,2,64,512]{3,2,1,0:T(8,128)(2,1)S(1)}, u32[]{:S(2)}, u32[]{:S(2)}) collective-permute-start(bf16[1,2,64,512]{3,2,1,0:T(8,128)(2,1)S(1)} %maximum_bitcast_fusion.refs_0_), channel_id=1, source_target_pairs={{0,1},{1,2},{2,3},{3,4},{4,5},{5,6},{6,7},{7,0},{8,9},{9,10},{10,1... | collective-permute-start | bytes 393224 | tf_op jit(solution)/shard_map/ppermute | solution.py:142
  25.3 4.5 %collective-permute-start.3 = (bf16[1,2,64,512]{3,2,1,0:T(8,128)(2,1)S(1)}, bf16[1,2,64,512]{3,2,1,0:T(8,128)(2,1)S(1)}, u32[]{:S(2)}, u32[]{:S(2)}) collective-permute-start(bf16[1,2,64,512]{3,2,1,0:T(8,128)(2,1)S(1)} %maximum_bitcast_fusion.refs_0_), channel_id=1, source_target_pairs={{0,7},{1,0},{2,1},{3,2},{4,3},{5,4},{6,5},{7,6},{8,15},{9,8},{10,9... | collective-permute-start | bytes 393224 | tf_op jit(solution)/shard_map/ppermute | solution.py:142
  30.4 0.1 pad_add_fusion.live_ref
  30.5 1.9 %collective-permute-done.1.refs_1_ = bf16[1,2,64,512]{3,2,1,0:T(8,128)(2,1)S(1)} collective-permute-done((bf16[1,2,64,512]{3,2,1,0:T(8,128)(2,1)S(1)}, bf16[1,2,64,512]{3,2,1,0:T(8,128)(2,1)S(1)}, u32[]{:S(2)}, u32[]{:S(2)}) %collective-permute-start.1) | collective-permute-done | bytes 131104 | tf_op jit(solution)/shard_map/ppermute | solution.py:142
  32.4 0.3 collective-permute-done.2.refs_2_
  32.7 0.0 collective-permute-done.3.refs_3_
  32.7 0.0 all-to-all-done.terms_ref
  32.7 0.0 copy-done.3
  32.7 0.0 copy-start.1
  32.7 0.0 copy-start.2
  32.7 1.5 %shard_map.96 = bf16[64,16,128]{2,1,0:T(8,128)(2,1)} custom-call(s32[64]{0:T(128)S(1)} %bitcast.21, bf16[8,32,16,128]{3,2,1,0:T(8,128)(2,1)S(1)} %all-to-all-done.terms_ref), custom_call_target="tpu_custom_call" | custom-call | tf_op jit(solution)/shard_map/pallas_call | solution.py:157
  34.2 12.5 %all-to-all-start.1 = ((bf16[64,16,128]{2,1,0:T(8,128)(2,1)}), bf16[64,16,128]{2,1,0:T(8,128)(2,1)S(1)}, u32[]{:S(2)}, u32[]{:S(2)}) async-start(bf16[64,16,128]{2,1,0:T(8,128)(2,1)} %shard_map.96), calls=%async_computation.1 | async-start | bytes 524288 | tf_op jit(solution)/shard_map/all_to_all | solution.py:168
  46.8 2.9 %collective-permute-start.4 = (bf16[2,2,64,512]{3,2,1,0:T(8,128)(2,1)S(1)}, bf16[2,2,64,512]{3,2,1,0:T(8,128)(2,1)S(1)}, u32[]{:S(2)}, u32[]{:S(2)}) collective-permute-start(bf16[2,2,64,512]{3,2,1,0:T(8,128)(2,1)S(1)} %get-tuple-element.28), channel_id=1, source_target_pairs={{0,1},{1,2},{2,3},{3,4},{4,5},{5,6},{6,7},{7,0},{8,9},{9,10},{10,1... | collective-permute-start | bytes 786440 | tf_op jit(solution)/shard_map/ppermute | solution.py:142
  49.7 4.6 %collective-permute-start.5 = (bf16[2,2,64,512]{3,2,1,0:T(8,128)(2,1)S(1)}, bf16[2,2,64,512]{3,2,1,0:T(8,128)(2,1)S(1)}, u32[]{:S(2)}, u32[]{:S(2)}) collective-permute-start(bf16[2,2,64,512]{3,2,1,0:T(8,128)(2,1)S(1)} %get-tuple-element.27), channel_id=1, source_target_pairs={{0,7},{1,0},{2,1},{3,2},{4,3},{5,4},{6,5},{7,6},{8,15},{9,8},{10,9... | collective-permute-start | bytes 786440 | tf_op jit(solution)/shard_map/ppermute | solution.py:142
  54.3 4.7 %collective-permute-done.4.refs_4_ = bf16[2,2,64,512]{3,2,1,0:T(8,128)(2,1)S(1)} collective-permute-done((bf16[2,2,64,512]{3,2,1,0:T(8,128)(2,1)S(1)}, bf16[2,2,64,512]{3,2,1,0:T(8,128)(2,1)S(1)}, u32[]{:S(2)}, u32[]{:S(2)}) %collective-permute-start.4) | collective-permute-done | bytes 262176 | tf_op jit(solution)/shard_map/ppermute | solution.py:142
  59.0 1.2 %collective-permute-done.5.refs_5_ = bf16[2,2,64,512]{3,2,1,0:T(8,128)(2,1)S(1)} collective-permute-done((bf16[2,2,64,512]{3,2,1,0:T(8,128)(2,1)S(1)}, bf16[2,2,64,512]{3,2,1,0:T(8,128)(2,1)S(1)}, u32[]{:S(2)}, u32[]{:S(2)}) %collective-permute-start.5) | collective-permute-done | bytes 262176 | tf_op jit(solution)/shard_map/ppermute | solution.py:142
  60.1 0.0 all-to-all-done.1.terms_ref
  60.1 0.1 shard_map.97
  60.2 21.7 %all_to_all.15.parts_ref = bf16[8,64,512]{2,1,0:T(8,128)(2,1)S(1)} all-to-all(bf16[8,64,512]{2,1,0:T(8,128)(2,1)S(1)} %shard_map.97), channel_id=1, replica_groups=mesh['zh'=4,'zl'=2,'x'=4,'c'=2,'mp'=8] {'mp'}, dimensions={0} | all-to-all | bytes 1048576 | tf_op jit(solution)/shard_map/all_to_all | solution.py:173
  82.0 0.0 copy-done.1
  82.0 0.0 copy-done.2
  82.0 2.6 %shard_map.98 = (bf16[64,512]{1,0:T(8,128)(2,1)}, bf16[64,512]{1,0:T(8,128)(2,1)}, bf16[64,512]{1,0:T(8,128)(2,1)}) custom-call(s32[2]{0:T(128)S(1)} %pad_add_fusion.live_ref, bf16[8,64,512]{2,1,0:T(8,128)(2,1)S(1)} %all_to_all.15.parts_ref, bf16[64,512]{1,0:T(8,128)(2,1)S(1)} %bitcast.19, bf16[64,512]{1,0:T(8,128)(2,1)S(1)} %bitcast.20, ...), custom_call_target="tpu_custom_call" | custom-call | tf_op jit(solution)/shard_map/pallas_call | solution.py:109
  (2 shorter events, 0.1 us)
Async XLA Ops:
  0.6 1.6 %copy-start = (bf16[1,32,64,512]{3,2,1,0:T(8,128)(2,1)S(1)}, bf16[1,32,64,512]{3,2,1,0:T(8,128)(2,1)}, u32[]{:S(2)}) copy-start(bf16[1,32,64,512]{3,2,1,0:T(8,128)(2,1)} %param.7) | copy-start | bytes 6291460
  2.4 4.6 %collective-permute-start = (bf16[32,32,512]{2,1,0:T(8,128)(2,1)S(1)}, bf16[32,32,512]{2,1,0:T(8,128)(2,1)S(1)}, u32[]{:S(2)}, u32[]{:S(2)}) collective-permute-start(bf16[32,32,512]{2,1,0:T(8,128)(2,1)S(1)} %shard_map.94), channel_id=1, source_target_pairs={{0,8},{8,0},{1,9},{9,1},{2,10},{10,2},{3,11},{11,3},{4,12},{12,4},... | collective-permute-start | bytes 3145736 | tf_op jit(solution)/shard_map/ppermute | solution.py:139
  8.2 9.5 %copy-start.4 = (bf16[1,1,512,64]{2,3,1,0:T(8,128)(2,1)S(1)}, bf16[1,1,512,64]{2,3,1,0:T(8,128)(2,1)}, u32[]{:S(2)}) copy-start(bf16[1,1,512,64]{2,3,1,0:T(8,128)(2,1)} %param.13) | copy-start | bytes 196612
  8.2 9.5 %copy-start.5 = (bf16[1,1,64,512]{3,2,1,0:T(8,128)(2,1)S(1)}, bf16[1,1,64,512]{3,2,1,0:T(8,128)(2,1)}, u32[]{:S(2)}) copy-start(bf16[1,1,64,512]{3,2,1,0:T(8,128)(2,1)} %param.12) | copy-start | bytes 196612
  8.2 24.5 %copy-start.3 = (s32[64,1]{0,1:T(1,128)S(1)}, s32[64,1]{0,1:T(1,128)}, u32[]{:S(2)}) copy-start(s32[64,1]{0,1:T(1,128)} %param.8) | copy-start | bytes 772
  8.2 24.5 %all-to-all-start = ((bf16[8,32,16,128]{3,2,1,0:T(8,128)(2,1)}), bf16[8,32,16,128]{3,2,1,0:T(8,128)(2,1)S(1)}, u32[]{:S(2)}, u32[]{:S(2)}) async-start(bf16[8,32,16,128]{3,2,1,0:T(8,128)(2,1)} %shard_map.95), calls=%async_computation | async-start | bytes 2097152 | tf_op jit(solution)/shard_map/all_to_all | solution.py:153
  17.7 14.7 %collective-permute-start.1 = (bf16[1,2,64,512]{3,2,1,0:T(8,128)(2,1)S(1)}, bf16[1,2,64,512]{3,2,1,0:T(8,128)(2,1)S(1)}, u32[]{:S(2)}, u32[]{:S(2)}) collective-permute-start(bf16[1,2,64,512]{3,2,1,0:T(8,128)(2,1)S(1)} %maximum_bitcast_fusion.refs_0_), channel_id=1, source_target_pairs={{0,4},{1,5},{2,6},{3,7},{4,0},{5,1},{6,2},{7,3},{8,12},{9,13},{10,... | collective-permute-start | bytes 393224 | tf_op jit(solution)/shard_map/ppermute | solution.py:142
  22.7 10.0 %collective-permute-start.2 = (bf16[1,2,64,512]{3,2,1,0:T(8,128)(2,1)S(1)}, bf16[1,2,64,512]{3,2,1,0:T(8,128)(2,1)S(1)}, u32[]{:S(2)}, u32[]{:S(2)}) collective-permute-start(bf16[1,2,64,512]{3,2,1,0:T(8,128)(2,1)S(1)} %maximum_bitcast_fusion.refs_0_), channel_id=1, source_target_pairs={{0,1},{1,2},{2,3},{3,4},{4,5},{5,6},{6,7},{7,0},{8,9},{9,10},{10,1... | collective-permute-start | bytes 393224 | tf_op jit(solution)/shard_map/ppermute | solution.py:142
  25.3 7.4 %collective-permute-start.3 = (bf16[1,2,64,512]{3,2,1,0:T(8,128)(2,1)S(1)}, bf16[1,2,64,512]{3,2,1,0:T(8,128)(2,1)S(1)}, u32[]{:S(2)}, u32[]{:S(2)}) collective-permute-start(bf16[1,2,64,512]{3,2,1,0:T(8,128)(2,1)S(1)} %maximum_bitcast_fusion.refs_0_), channel_id=1, source_target_pairs={{0,7},{1,0},{2,1},{3,2},{4,3},{5,4},{6,5},{7,6},{8,15},{9,8},{10,9... | collective-permute-start | bytes 393224 | tf_op jit(solution)/shard_map/ppermute | solution.py:142
  32.7 49.3 %copy-start.1 = (bf16[1,1,64,512]{3,2,1,0:T(8,128)(2,1)S(1)}, bf16[1,1,64,512]{3,2,1,0:T(8,128)(2,1)}, u32[]{:S(2)}) copy-start(bf16[1,1,64,512]{3,2,1,0:T(8,128)(2,1)} %param.10) | copy-start | bytes 196612
  32.7 49.3 %copy-start.2 = (bf16[1,1,64,512]{3,2,1,0:T(8,128)(2,1)S(1)}, bf16[1,1,64,512]{3,2,1,0:T(8,128)(2,1)}, u32[]{:S(2)}) copy-start(bf16[1,1,64,512]{3,2,1,0:T(8,128)(2,1)} %param.11) | copy-start | bytes 196612
  34.2 25.9 %all-to-all-start.1 = ((bf16[64,16,128]{2,1,0:T(8,128)(2,1)}), bf16[64,16,128]{2,1,0:T(8,128)(2,1)S(1)}, u32[]{:S(2)}, u32[]{:S(2)}) async-start(bf16[64,16,128]{2,1,0:T(8,128)(2,1)} %shard_map.96), calls=%async_computation.1 | async-start | bytes 524288 | tf_op jit(solution)/shard_map/all_to_all | solution.py:168
  46.8 12.2 %collective-permute-start.4 = (bf16[2,2,64,512]{3,2,1,0:T(8,128)(2,1)S(1)}, bf16[2,2,64,512]{3,2,1,0:T(8,128)(2,1)S(1)}, u32[]{:S(2)}, u32[]{:S(2)}) collective-permute-start(bf16[2,2,64,512]{3,2,1,0:T(8,128)(2,1)S(1)} %get-tuple-element.28), channel_id=1, source_target_pairs={{0,1},{1,2},{2,3},{3,4},{4,5},{5,6},{6,7},{7,0},{8,9},{9,10},{10,1... | collective-permute-start | bytes 786440 | tf_op jit(solution)/shard_map/ppermute | solution.py:142
  49.7 10.4 %collective-permute-start.5 = (bf16[2,2,64,512]{3,2,1,0:T(8,128)(2,1)S(1)}, bf16[2,2,64,512]{3,2,1,0:T(8,128)(2,1)S(1)}, u32[]{:S(2)}, u32[]{:S(2)}) collective-permute-start(bf16[2,2,64,512]{3,2,1,0:T(8,128)(2,1)S(1)} %get-tuple-element.27), channel_id=1, source_target_pairs={{0,7},{1,0},{2,1},{3,2},{4,3},{5,4},{6,5},{7,6},{8,15},{9,8},{10,9... | collective-permute-start | bytes 786440 | tf_op jit(solution)/shard_map/ppermute | solution.py:142
